TPU v7x, 32 devices: a whole 2x2x4 slice. The times are simulated.
32 devices in a mesh: blk: 16 (over z, y, core), shard: 2 (over x).
Axes of the slice: x: 2, y: 2, z: 4, core: 2. Of those that a mesh axis runs over, the one named last changes fastest.
Arguments:
- features: bfloat16 [2, 16384, 2048], P(None, ('blk', 'shard')), may hold values from -6 to 6
- weight: bfloat16 [2048, 2048], P(('blk', 'shard')), may hold values from -0.125 to 0.125
- bias: bfloat16 [2048], P(('blk', 'shard')), may hold values from -3 to 3
- cotangent: bfloat16 [2, 16384, 2048], P(None, ('blk', 'shard')), may hold values from -6 to 6
- neighbours: int32 [2, 16384, 16], P(None, ('blk', 'shard')), may hold values from -1 to 895, as said below
- live_count: int32 [2, 32], P(None, ('blk', 'shard')), may hold values from 128 to 512, as said below
Outputs:
- activated: bfloat16 [2, 16384, 2048], P(None, ('blk', 'shard'))
- feature_grad: bfloat16 [2, 16384, 2048], P(None, ('blk', 'shard'))
- weight_grad: float32 [2048, 2048], P(('blk', 'shard'))
- bias_grad: float32 [2048], P(('blk', 'shard'))
Inputs may be any that keep to these rules, and one draw needn't show every extreme that they name: `neighbours`: for each slot, 16 entries in any order: -1 for an empty entry; c < the slot's live count for row c of the same device; 512 + s * 64 + r for row r of the device with shard index s in the same blk group; that plus 2 * 64 for the group before on the cycle (blk index minus 1, cyclic); that plus 2 * 2 * 64 for the group after. Slots at or beyond their device's live count hold only -1. `live_count`: devices are numbered blk-major. Each micro-batch has some device with all 512 slots live.
All inputs are finite; a program needn't handle non-finite values.
Results may differ from a plain program's by a relative error of at most 0.0059.
Values may be sent and summed in bfloat16 or wider, within the bound.
No kernel may reach another device: no remote copies, remote signals or barrier semaphores. Data moves between devices by JAX's collectives and lax.ppermute only.
A program may use at most 72 MiB of HBM per device.

v0:
```python
import jax
import jax.numpy as jnp
from jax import lax
from jax.sharding import PartitionSpec as P


def from_behind(shard, axis, by):
    count = lax.axis_size(axis)
    return lax.ppermute(shard, axis, [(i, (i + by) % count) for i in range(count)])


def count_table(lookup, usable, table_rows, block_rows):
    node_count, fanout = lookup.shape
    block_count = node_count // block_rows
    columns = jnp.arange(table_rows, dtype=jnp.int32)

    def one_block(packed):
        look, usage = packed
        hits = (look[:, :, None] == columns[None, None, :]).astype(jnp.float32) * usage[:, :, None]
        return jnp.sum(hits, axis=1)

    packed = (
        lookup.reshape(block_count, block_rows, fanout),
        usable.reshape(block_count, block_rows, fanout),
    )
    return lax.map(one_block, packed).reshape(node_count, table_rows)


def reduce_grads(weight_term, bias_term):
    return (
        lax.psum_scatter(weight_term, ("blk", "shard"), scatter_dimension=0, tiled=True),
        lax.psum_scatter(bias_term, ("blk", "shard"), scatter_dimension=0, tiled=True),
    )


def per_device(features, weight, bias, cotangent, neighbours, live_count):
    micro_count, node_count, width = features.shape
    rim_size = node_count // 8
    block_rows = min(128, node_count)
    outputs = []
    input_grads = []
    weight_sum = None
    bias_sum = None
    for micro in range(micro_count):
        weight_full, bias_full = (
            lax.all_gather(weight, ("blk", "shard"), axis=0, tiled=True),
            lax.all_gather(bias, ("blk", "shard"), axis=0, tiled=True),
        )
        own_rows = features[micro]
        rim_rows = own_rows[:rim_size]
        group_rims = lax.all_gather(rim_rows, "shard", axis=0, tiled=True)
        rims_before = from_behind(group_rims, "blk", 1)
        rims_after = from_behind(group_rims, "blk", -1)
        group_size = group_rims.shape[0]
        source_rows = jnp.concatenate([own_rows, group_rims, rims_before, rims_after], axis=0)
        entries = neighbours[micro]
        usable = (entries >= 0).astype(jnp.float32)
        lookup = jnp.where(entries >= 0, entries, 0)
        degree = jnp.sum(usable, axis=1)
        alive = (jnp.arange(node_count, dtype=jnp.int32) < live_count[micro, 0]).astype(jnp.float32)
        weighting = alive / (degree + 1.0)
        counts = count_table(lookup, usable, source_rows.shape[0], block_rows)
        summed = jnp.dot(
            counts.astype(jnp.bfloat16), source_rows, preferred_element_type=jnp.float32
        )
        mixed = (summed + 2.0 * own_rows.astype(jnp.float32)) * weighting[:, None]
        mixed_low = mixed.astype(jnp.bfloat16)
        linear = jnp.dot(
            mixed_low, weight_full, preferred_element_type=jnp.float32
        ) + bias_full.astype(jnp.float32)
        outputs.append((jax.nn.gelu(linear) * alive[:, None]).astype(jnp.bfloat16))
        incoming = cotangent[micro].astype(jnp.float32) * alive[:, None]
        _, gelu_pull = jax.vjp(jax.nn.gelu, linear)
        linear_grad = gelu_pull(incoming)[0].astype(jnp.bfloat16)
        weight_term = jnp.einsum(
            "nd,ne->de", mixed_low, linear_grad, preferred_element_type=jnp.float32
        )
        bias_term = jnp.sum(linear_grad.astype(jnp.float32), axis=0)
        mixed_grad = jnp.einsum(
            "ne,de->nd", linear_grad, weight_full, preferred_element_type=jnp.float32
        ).astype(jnp.bfloat16)
        scaled_grad = mixed_grad.astype(jnp.float32) * weighting[:, None]
        table_grad = jnp.einsum(
            "nt,nd->td",
            counts,
            scaled_grad,
            precision=lax.Precision.HIGHEST,
            preferred_element_type=jnp.float32,
        )
        local_grad = table_grad[:node_count] + 2.0 * scaled_grad
        group_grad = table_grad[node_count : node_count + group_size]
        before_grad = table_grad[node_count + group_size : node_count + 2 * group_size]
        after_grad = table_grad[node_count + 2 * group_size :]
        back_before = from_behind(before_grad.astype(jnp.bfloat16), "blk", -1).astype(
            before_grad.dtype
        )
        back_after = from_behind(after_grad.astype(jnp.bfloat16), "blk", 1).astype(after_grad.dtype)
        rim_grad = lax.psum_scatter(
            group_grad + back_before + back_after, "shard", scatter_dimension=0, tiled=True
        )
        local_grad = local_grad.at[:rim_size].add(rim_grad)
        input_grads.append(local_grad.astype(jnp.bfloat16))
        weight_piece, bias_piece = reduce_grads(weight_term, bias_term)
        weight_sum = weight_piece if weight_sum is None else weight_sum + weight_piece
        bias_sum = bias_piece if bias_sum is None else bias_sum + bias_piece
    return (jnp.stack(outputs), jnp.stack(input_grads), weight_sum, bias_sum)


def solution(mesh):
    in_specs = (
        P(None, ("blk", "shard"), None),
        P(("blk", "shard"), None),
        P(("blk", "shard")),
        P(None, ("blk", "shard"), None),
        P(None, ("blk", "shard"), None),
        P(None, ("blk", "shard")),
    )
    out_specs = (
        P(None, ("blk", "shard"), None),
        P(None, ("blk", "shard"), None),
        P(("blk", "shard"), None),
        P(("blk", "shard")),
    )
    return jax.shard_map(
        per_device, mesh=mesh, in_specs=in_specs, out_specs=out_specs, check_vma=False
    )
```

profile of v0, /device:TPU:0, one launch (start us, length us, event | category | flops | bytes accessed | tf_op | source)
XLA Modules:
  0.0 607.4 jit_solution(15731345360677799162)
XLA Ops:
  9.0 9.9 %all-gather.1 = bf16[1,128,2048]{2,1,0:T(8,128)(2,1)S(1)} all-gather(bf16[1,64,2048]{2,1,0:T(8,128)(2,1)S(1)} %get-tuple-element.156), channel_id=3, replica_groups=mesh['blk'=16,'shard'=2] {'shard'}, dimensions={1}, use_global_device_ids=true | all-gather | bytes 786432 | tf_op jit(solution)/shard_map/all_gather | solution.py:51
  18.9 3.4 collective-permute-start.3
  22.3 9.3 %all-gather = bf16[1,128,2048]{2,1,0:T(8,128)(2,1)S(1)} all-gather(bf16[1,64,2048]{2,1,0:T(8,128)(2,1)S(1)} %get-tuple-element.155), channel_id=2, replica_groups=mesh['blk'=16,'shard'=2] {'shard'}, dimensions={1}, use_global_device_ids=true | all-gather | bytes 786432 | tf_op jit(solution)/shard_map/all_gather | solution.py:51
  31.6 4.2 collective-permute-start.1
  36.7 46.2 %all-reduce = bf16[2048]{0:T(1024)(128)(2,1)S(1)} all-reduce(bf16[2048]{0:T(1024)(128)(2,1)S(1)} %dynamic-update-slice.6), channel_id=1, replica_groups=mesh['blk'=16,'shard'=2] {'blk','shard'}, use_global_device_ids=true, to_apply=%add | all-reduce | flops 2048 | bytes 8192
  89.9 11.4 %while.24 = (s32[]{:T(128)}, f32[4,128,896]{2,1,0:T(8,128)}, s32[4,128,16]{1,0,2:T(4,128)S(1)}, f32[4,128,16]{1,0,2:T(4,128)S(1)}, s32[]{:T(128)}) while((s32[]{:T(128)}, f32[4,128,896]{2,1,0:T(8,128)}, s32[4,128,16]{1,0,2:T(4,128)S(1)}, f32[4,128,16]{1,0,2:T(4,128)S(1)}, s32[]{:T(128)}) %tuple.72), condition=%wide.region_2.3_spmd.clone, body=%wide.region_0.0_spmd.clone.sunk | while | flops 5390338 | bytes 1458257 | solution.py:26
  90.1 1.8 select_reduce_fusion.4
  93.0 1.8 select_reduce_fusion.4
  101.4 8.4 %while.25 = (s32[]{:T(128)}, f32[4,128,896]{2,1,0:T(8,128)S(1)}, s32[4,128,16]{1,0,2:T(4,128)S(1)}, f32[4,128,16]{1,0,2:T(4,128)S(1)}, s32[]{:T(128)}) while((s32[]{:T(128)}, f32[4,128,896]{2,1,0:T(8,128)S(1)}, s32[4,128,16]{1,0,2:T(4,128)S(1)}, f32[4,128,16]{1,0,2:T(4,128)S(1)}, s32[]{:T(128)}) %tuple.75), condition=%wide.region_6.7_spmd.clone, body=%wide.region_4.6_spmd.clone.sunk | while | flops 5390338 | bytes 1458257 | solution.py:26
  101.6 1.8 select_reduce_fusion.5
  109.8 2.7 slice_bitcast_fusion.1
  112.5 5.5 multiply_convert_fusion.3
  118.0 4.9 multiply_convert_fusion.1
  123.0 10.7 %fusion.73 = f32[512,2048]{1,0:T(8,128)} fusion(bf16[512,2048]{1,0:T(8,128)(2,1)} %multiply_convert_fusion.3, bf16[2048,2048]{1,0:T(8,128)(2,1)} %all-gather.4.cloned.1.call-done), kind=kOutput, calls=%fused_computation.114 | convolution fusion | flops 4294967296 | bytes 14680064 | tf_op jit(solution)/shard_map/dot_general | solution.py:68
  133.7 15.6 %convert_reduce_fusion.1 = (f32[2048]{0:T(1024)S(1)}, bf16[512,2048]{1,0:T(8,128)(2,1)S(1)}, bf16[1,512,2048]{2,1,0:T(8,128)(2,1)}, bf16[1,512,2048]{2,1,0:T(8,1...) fusion(f32[512,2048]{1,0:T(8,128)} %fusion.73, f32[2048]{0:T(1024)S(1)} %convert_element_type.128, ...), kind=kOutput, calls=%fused_computation.48 | convolution fusion | flops 4353683456 | bytes 27291648 | tf_op jit(solution)/shard_map/dot_general | solution.py:68
  149.2 4.8 convolution_convert_fusion
  154.1 13.6 %fusion.71 = (bf16[896,2048]{1,0:T(8,128)(2,1)S(1)}, f32[896,2048]{1,0:T(8,128)S(1)}) fusion(f32[512,896]{1,0:T(8,128)S(1)} %bitcast.75, bf16[512,2048]{1,0:T(8,128)(2,1)S(1)} %convolution_convert_fusion, f32[512]{0:T(512)S(1)} %add_divide_fusion), kind=kOutput, calls=%fused_computation.112 | convolution fusion | flops 11278221312 | bytes 14944256 | tf_op jit(solution)/shard_map/nt,nd->td/dot_general | solution.py:83
  169.4 8.9 %convolution_convert_fusion.1 = bf16[512,2048]{1,0:T(8,128)(2,1)S(1)} fusion(bf16[512,2048]{1,0:T(8,128)(2,1)S(1)} %get-tuple-element.149, bf16[2048,2048]{1,0:T(8,128)(2,1)} %all-gather.4.cloned.1.call-done), kind=kOutput, calls=%fused_computation.74 | convolution fusion | flops 4296015872 | bytes 12582912 | tf_op jit(solution)/shard_map/ne,de->nd/dot_general | solution.py:79
  178.3 16.3 %fusion.72 = (bf16[896,2048]{1,0:T(8,128)(2,1)}, f32[896,2048]{1,0:T(8,128)}) fusion(f32[512,896]{1,0:T(8,128)} %bitcast, bf16[512,2048]{1,0:T(8,128)(2,1)S(1)} %convolution_convert_fusion.1, f32[512]{0:T(512)S(1)} %add_divide_fusion.1), kind=kOutput, calls=%fused_computation.113 | convolution fusion | flops 11278221312 | bytes 14944256 | tf_op jit(solution)/shard_map/nt,nd->td/dot_general | solution.py:83
  197.1 3.8 collective-permute-start.4
  201.1 12.9 %fusion.74 = f32[2048,2048]{1,0:T(8,128)} fusion(bf16[512,2048]{1,0:T(8,128)(2,1)} %multiply_convert_fusion.3, bf16[512,2048]{1,0:T(8,128)(2,1)} %copy-done.8), kind=kOutput, calls=%fused_computation.115 | convolution fusion | flops 4294967296 | bytes 20971520 | tf_op jit(solution)/shard_map/nd,ne->de/dot_general | solution.py:75
  213.9 2.4 fusion.55
  216.4 17.4 %convolution_add_fusion = f32[2048,2048]{1,0:T(8,128)} fusion(f32[2048,2048]{1,0:T(8,128)} %fusion.74, bf16[512,2048]{1,0:T(8,128)(2,1)} %multiply_convert_fusion.1, bf16[512,2048]{1,0:T(8,128)(2,1)} %copy-done.5), kind=kOutput, calls=%fused_computation.12 | convolution fusion | flops 4299161600 | bytes 37748736 | tf_op jit(solution)/shard_map/nd,ne->de/dot_general | solution.py:75
  233.9 40.4 %all-reduce.1 = f32[2048]{0:T(1024)S(1)} all-reduce(f32[2048]{0:T(1024)S(1)} %add.130), channel_id=9, replica_groups=mesh['blk'=16,'shard'=2] {'blk','shard'}, use_global_device_ids=true, to_apply=%region_13.14.clone | all-reduce | flops 2048 | bytes 16384
  274.8 4.8 pad_maximum_fusion
  279.6 5.0 slice_add_fusion
  284.6 2.6 slice_add_fusion.1
  287.2 2.0 fusion.58
  289.2 2.1 fusion.59
  291.3 2.7 convert_bitcast_fusion
  295.1 2.4 pad_maximum_fusion.1
  297.5 303.1 %reduce-scatter.8.cloned.1.call-done = f32[64,2048]{1,0:T(8,128)} async-done(((f32[2048,2048]{1,0:T(8,128)}), f32[64,2048]{1,0:T(8,128)}) %reduce-scatter.8.cloned.1.call-update) | async-done | bytes 524304 | tf_op jit(solution)/shard_map/reduce_scatter | solution.py:31
  (116 shorter events, 30.1 us)
Async XLA Ops:
  7.2 115.8 %all-gather.4.cloned.1.call-start = ((), (), s32[]{:S(2)}) async-start(), calls=%async_computation.3 | async-start | bytes 8650752 | tf_op jit(solution)/shard_map/all_gather | solution.py:46
  7.9 279.3 %reduce-scatter.6.cloned.1.call-start = ((), (), s32[]{:S(2)}) async-start(), calls=%async_computation.5 | async-start | bytes 1572864 | tf_op jit(solution)/shard_map/reduce_scatter | solution.py:98
  18.9 99.1 %collective-permute-start.3 = (bf16[128,2048]{1,0:T(8,128)(2,1)S(1)}, bf16[128,2048]{1,0:T(8,128)(2,1)}, u32[]{:S(2)}, u32[]{:S(2)}) collective-permute-start(bf16[128,2048]{1,0:T(8,128)(2,1)S(1)} %bitcast.80), channel_id=1, source_target_pairs={{0,30},{2,0},{4,2},{6,4},{8,6},{10,8},{12,10},{14,12},{16,14},{18,... | collective-permute-start | bytes 1572872 | tf_op jit(solution)/shard_map/ppermute | solution.py:9
  22.3 95.7 %collective-permute-start.2 = (bf16[128,2048]{1,0:T(8,128)(2,1)S(1)}, bf16[128,2048]{1,0:T(8,128)(2,1)}, u32[]{:S(2)}, u32[]{:S(2)}) collective-permute-start(bf16[128,2048]{1,0:T(8,128)(2,1)S(1)} %bitcast.81), channel_id=1, source_target_pairs={{0,2},{2,4},{4,6},{6,8},{8,10},{10,12},{12,14},{14,16},{16,18},{18... | collective-permute-start | bytes 1572872 | tf_op jit(solution)/shard_map/ppermute | solution.py:9
  31.6 80.9 %collective-permute-start.1 = (bf16[128,2048]{1,0:T(8,128)(2,1)S(1)}, bf16[128,2048]{1,0:T(8,128)(2,1)}, u32[]{:S(2)}, u32[]{:S(2)}) collective-permute-start(bf16[128,2048]{1,0:T(8,128)(2,1)S(1)} %bitcast.83), channel_id=1, source_target_pairs={{0,30},{2,0},{4,2},{6,4},{8,6},{10,8},{12,10},{14,12},{16,14},{18,... | collective-permute-start | bytes 1572872 | tf_op jit(solution)/shard_map/ppermute | solution.py:9
  35.8 76.7 %collective-permute-start = (bf16[128,2048]{1,0:T(8,128)(2,1)S(1)}, bf16[128,2048]{1,0:T(8,128)(2,1)}, u32[]{:S(2)}, u32[]{:S(2)}) collective-permute-start(bf16[128,2048]{1,0:T(8,128)(2,1)S(1)} %bitcast.84), channel_id=1, source_target_pairs={{0,2},{2,4},{4,6},{6,8},{8,10},{10,12},{12,14},{14,16},{16,18},{18... | collective-permute-start | bytes 1572872 | tf_op jit(solution)/shard_map/ppermute | solution.py:9
  123.0 10.7 %copy-start.4 = (bf16[512,2048]{1,0:T(8,128)(2,1)S(1)}, bf16[512,2048]{1,0:T(8,128)(2,1)}, u32[]{:S(2)}) copy-start(bf16[512,2048]{1,0:T(8,128)(2,1)} %multiply_convert_fusion.1) | copy-start | bytes 6291460
  123.0 10.7 %copy-start.6 = (bf16[2048,2048]{1,0:T(8,128)(2,1)S(1)}, bf16[2048,2048]{1,0:T(8,128)(2,1)}, u32[]{:S(2)}) copy-start(bf16[2048,2048]{1,0:T(8,128)(2,1)} %all-gather.4.cloned.1.call-done) | copy-start | bytes 25165828
  123.0 10.7 %copy-start.7 = (bf16[2,512,2048]{2,1,0:T(8,128)(2,1)S(1)}, bf16[2,512,2048]{2,1,0:T(8,128)(2,1)}, u32[]{:S(2)}) copy-start(bf16[2,512,2048]{2,1,0:T(8,128)(2,1)} %param.17) | copy-start | bytes 12582916
  149.2 4.8 copy-start.5
  149.2 20.2 %copy-start.8 = (bf16[512,2048]{1,0:T(8,128)(2,1)}, bf16[512,2048]{1,0:T(8,128)(2,1)S(1)}, u32[]{:S(2)}) copy-start(bf16[512,2048]{1,0:T(8,128)(2,1)S(1)} %get-tuple-element.149) | copy-start | bytes 6291460
  154.0 13.6 %copy-start.2 = (bf16[512,2048]{1,0:T(8,128)(2,1)}, bf16[512,2048]{1,0:T(8,128)(2,1)S(1)}, u32[]{:S(2)}) copy-start(bf16[512,2048]{1,0:T(8,128)(2,1)S(1)} %convolution_convert_fusion) | copy-start | bytes 6291460
  167.6 27.0 %copy-start = (f32[896,2048]{1,0:T(8,128)}, f32[896,2048]{1,0:T(8,128)S(1)}, u32[]{:S(2)}) copy-start(f32[896,2048]{1,0:T(8,128)S(1)} %get-tuple-element.168) | copy-start | bytes 22020100
  167.8 26.8 %collective-permute-start.6 = (bf16[128,2048]{1,0:T(8,128)(2,1)S(1)}, bf16[128,2048]{1,0:T(8,128)(2,1)S(1)}, u32[]{:S(2)}, u32[]{:S(2)}) collective-permute-start(bf16[128,2048]{1,0:T(8,128)(2,1)S(1)} %get-tuple-element.161), channel_id=1, source_target_pairs={{0,30},{2,0},{4,2},{6,4},{8,6},{10,8},{12,10},{14,12},{16,14},{18,... | collective-permute-start | bytes 1572872 | tf_op jit(solution)/shard_map/ppermute | solution.py:9
  169.4 25.2 %collective-permute-start.7 = (bf16[128,2048]{1,0:T(8,128)(2,1)S(1)}, bf16[128,2048]{1,0:T(8,128)(2,1)S(1)}, u32[]{:S(2)}, u32[]{:S(2)}) collective-permute-start(bf16[128,2048]{1,0:T(8,128)(2,1)S(1)} %get-tuple-element.162), channel_id=1, source_target_pairs={{0,2},{2,4},{4,6},{6,8},{8,10},{10,12},{12,14},{14,16},{16,18},{18... | collective-permute-start | bytes 1572872 | tf_op jit(solution)/shard_map/ppermute | solution.py:9
  195.7 93.5 %reduce-scatter.4.cloned.1.call-start = ((), (), s32[]{:S(2)}) async-start(), calls=%async_computation.4 | async-start | bytes 1572864 | tf_op jit(solution)/shard_map/reduce_scatter | solution.py:98
  197.1 16.8 %collective-permute-start.4 = (bf16[128,2048]{1,0:T(8,128)(2,1)S(1)}, bf16[128,2048]{1,0:T(8,128)(2,1)S(1)}, u32[]{:S(2)}, u32[]{:S(2)}) collective-permute-start(bf16[128,2048]{1,0:T(8,128)(2,1)S(1)} %get-tuple-element.159), channel_id=1, source_target_pairs={{0,30},{2,0},{4,2},{6,4},{8,6},{10,8},{12,10},{14,12},{16,14},{18,... | collective-permute-start | bytes 1572872 | tf_op jit(solution)/shard_map/ppermute | solution.py:9
  200.9 13.1 %collective-permute-start.5 = (bf16[128,2048]{1,0:T(8,128)(2,1)S(1)}, bf16[128,2048]{1,0:T(8,128)(2,1)S(1)}, u32[]{:S(2)}, u32[]{:S(2)}) collective-permute-start(bf16[128,2048]{1,0:T(8,128)(2,1)S(1)} %get-tuple-element.160), channel_id=1, source_target_pairs={{0,2},{2,4},{4,6},{6,8},{8,10},{10,12},{12,14},{14,16},{16,18},{18... | collective-permute-start | bytes 1572872 | tf_op jit(solution)/shard_map/ppermute | solution.py:9
  216.4 384.2 %reduce-scatter.8.cloned.1.call-start = ((), (), s32[]{:S(2)}) async-start(), calls=%async_computation.6 | async-start | bytes 17301504 | tf_op jit(solution)/shard_map/reduce_scatter | solution.py:31
  274.8 4.8 copy-start.3
  274.8 9.8 %slice-start = ((s8[7340032]{0:T(1024)(128)(4,1)}), s8[3145728]{0:T(1024)(128)(4,1)S(1)}, s32[]{:S(2)}) async-start(s8[7340032]{0:T(1024)(128)(4,1)} %bitcast.72), calls=%async_computation.7 | async-start | bytes 6291456
  279.6 5.0 slice-start.1
  291.3 3.5 copy-start.1
Sparse Core Ops, SparseCore 0:
  11.0 85.8 all-gather.3
  195.9 21.1 reduce-scatter.5
  219.4 20.4 reduce-scatter.3
  242.6 357.8 reduce-scatter.7
where the time goes:
time: 617 us; the launch traced here: 607 us
  waiting for transfers between devices  304 us (49%)
  matrix products  110 us (18%)
  blocking collectives  106 us (17%)
  other arithmetic  43.1 us (7%)
  local copies, waits for them, and re-layouts  16.3 us (3%)
  between operations  14.3 us (2%)
  starting transfers between devices  13.4 us (2%)
    reduce_scatter x1, waiting for transfers between devices, reduce_grads(): lax.psum_scatter(weight_term, ('blk', 'shard'), scatter_dimension=0, tile...  303 us
    unnamed x2, blocking collectives  86.6 us
    dot_general x2, matrix products, per_device(): jnp.einsum('nd,ne->de', mixed_low, linear_grad, preferred_element_type=jn...  30.2 us
    dot_general x2, matrix products, per_device(): jnp.einsum('nt,nd->td', counts, scaled_grad, precision=lax.Precision.HIGH...  29.9 us
    dot_general x2, matrix products, per_device(): jnp.dot(mixed_low, weight_full, preferred_element_type=jnp.float32)  26.2 us
    all_gather x2, blocking collectives, per_device(): group_rims = lax.all_gather(rim_rows, 'shard', axis=0, tiled=True)  19.2 us
    reduce_sum x8, other arithmetic, one_block(): return jnp.sum(hits, axis=1)  14.2 us
    dot_general x2, matrix products, per_device(): jnp.einsum('ne,de->nd', linear_grad, weight_full, preferred_element_type=...  13.7 us
  transfers between devices with their start and end apart: 12, of which 1 were waited for; matrix products, arithmetic and copies ran while one was open for 20% of the time, Pallas kernels for 0%

commit v1 on v0

v1 whole, which is shorter than its diff:
```python
import functools

import jax
import jax.numpy as jnp
import numpy as np
from jax import lax
from jax.experimental import pallas as pl
from jax.experimental.pallas import tpu as pltpu
from jax.sharding import PartitionSpec as P

BOTH = ("blk", "shard")
F32 = jnp.float32
BF16 = jnp.bfloat16
MIB = 1 << 20
GELU_A = 0.7978845608028654
GELU_B = 0.044715
ANY = pl.BlockSpec(memory_space=pl.ANY)
VMEM = pl.BlockSpec(memory_space=pltpu.VMEM)
SMEM = pl.BlockSpec(memory_space=pltpu.SMEM)

CHUNKS = (0.5, 0.5)
GATHER_ORDER = (("zxy", "zyx"), ("zxy", "zyx"))
REDUCE_ORDER = (("xyz", "yxz"), ("xyz", "yxz"))


def small_dot(a, b, contract=((1,), (0,))):
    return lax.dot_general(a, b, (contract, ((), ())), preferred_element_type=F32)


def count_kernel(rows, code_ref, code_t_ref, cnt_ref, cnt_t_ref):
    node_count, slots = code_ref.shape
    table = cnt_ref.shape[1]
    step = 32

    def by_node(i, carry):
        at = pl.ds(pl.multiple_of(i * step, step), step)
        codes = code_ref[at, :]
        column = lax.broadcasted_iota(jnp.int32, (step, table), 1)
        row = lax.broadcasted_iota(jnp.int32, (step, table), 0) + i * step
        total = jnp.where(column == row, 2.0, 0.0)
        for k in range(slots):
            total = total + jnp.where(column == codes[:, k : k + 1], 1.0, 0.0)
        cnt_ref[at, :] = total.astype(BF16)
        return carry

    def by_entry(i, carry):
        at = pl.ds(pl.multiple_of(i * step, step), step)
        row = lax.broadcasted_iota(jnp.int32, (step, node_count), 0) + i * step
        column = lax.broadcasted_iota(jnp.int32, (step, node_count), 1)
        total = jnp.where(column == row, 2.0, 0.0)
        for k in range(slots):
            total = total + jnp.where(row == code_t_ref[k : k + 1, :], 1.0, 0.0)
        cnt_t_ref[at, :] = total.astype(BF16)
        return carry

    lax.fori_loop(0, node_count // step, by_node, 0)
    lax.fori_loop(0, table // step, by_entry, 0)


def count_tables(codes, table):
    micro, node_count, slots = codes.shape
    return pl.pallas_call(
        functools.partial(count_kernel, node_count),
        grid=(micro,),
        in_specs=[
            pl.BlockSpec((None, node_count, slots), lambda m: (m, 0, 0)),
            pl.BlockSpec((None, slots, node_count), lambda m: (m, 0, 0)),
        ],
        out_specs=[
            pl.BlockSpec((None, node_count, table), lambda m: (m, 0, 0)),
            pl.BlockSpec((None, table, node_count), lambda m: (m, 0, 0)),
        ],
        out_shape=[
            jax.ShapeDtypeStruct((micro, node_count, table), BF16),
            jax.ShapeDtypeStruct((micro, table, node_count), BF16),
        ],
        compiler_params=pltpu.CompilerParams(vmem_limit_bytes=24 * MIB),
        name="count_tables",
    )(codes, jnp.swapaxes(codes, 1, 2))


def mix_kernel(cnt_ref, scale_ref, own_ref, *refs):
    piece_refs, (mixed_ref, mixed_t_ref, rim) = refs[:-3], refs[-3:]
    node_count = own_ref.shape[0]
    at = 0
    for piece in piece_refs:
        rim[at : at + piece.shape[0], :] = piece[...]
        at += piece.shape[0]
    total = small_dot(cnt_ref[:, :node_count], own_ref[...])
    total = total + small_dot(cnt_ref[:, node_count:], rim[...])
    scale = jnp.concatenate([scale_ref[...]] * (total.shape[1] // 128), axis=1)
    low = (total * scale).astype(BF16)
    mixed_ref[...] = low
    mixed_t_ref[...] = low.T


def mix(cnt, scale, features, pieces):
    micro, node_count, width = features.shape
    table = cnt.shape[2]
    wide = min(512, width)

    def along(rows):
        return pl.BlockSpec((None, rows, wide), lambda m, j: (m, 0, j))

    return pl.pallas_call(
        mix_kernel,
        grid=(micro, width // wide),
        in_specs=[
            pl.BlockSpec((None, node_count, table), lambda m, j: (m, 0, 0)),
            pl.BlockSpec((node_count, 128), lambda m, j: (m, 0)),
            along(node_count),
        ]
        + [along(piece.shape[1]) for piece in pieces],
        out_specs=[
            pl.BlockSpec((node_count, wide), lambda m, j: (m, j)),
            pl.BlockSpec((wide, node_count), lambda m, j: (j, m)),
        ],
        out_shape=[
            jax.ShapeDtypeStruct((micro * node_count, width), BF16),
            jax.ShapeDtypeStruct((width, micro * node_count), BF16),
        ],
        scratch_shapes=[pltpu.VMEM((table - node_count, wide), BF16)],
        compiler_params=pltpu.CompilerParams(vmem_limit_bytes=24 * MIB),
        name="mix",
    )(cnt, scale, features, *pieces)


def gelu_and_grad(linear, incoming, alive):
    square = linear * linear
    bend = jnp.tanh(linear * (GELU_A + (GELU_A * GELU_B) * square))
    share = 0.5 + 0.5 * bend
    value = linear * share
    slope = share + value * (1.0 - bend) * (GELU_A + (3.0 * GELU_A * GELU_B) * square)
    return (value * alive).astype(BF16), (incoming.astype(F32) * alive * slope).astype(BF16)


def layer_kernel(plan, *refs):
    start, size, first, last, piece_plan, tile, sub, block = plan
    n_pieces = len(piece_plan)
    (place_ref, slot_ref, half_ref, mixed, mixed_t, bias, cot, alive, scale) = refs[:9]
    pieces = refs[9 : 9 + n_pieces]
    rest = refs[9 + n_pieces :]
    acc_in = None
    if not first:
        acc_in, rest = rest[0], rest[2:]
    (act, send, keep, bias_grad, acc_out) = rest[:5]
    (wv, cv, av, lv, gv, linear, acc_a, acc_b, sem) = rest[5:]
    half = size // 2
    node_count = mixed.shape[0]
    width = mixed.shape[1]
    per = half // tile
    mine = half_ref[0]
    offsets = [
        pl.multiple_of(start + (1 - mine) * half, 128),
        pl.multiple_of(start + mine * half, 128),
    ]

    at = 0
    for ref, (side, count, rows) in zip(pieces, piece_plan):
        for i in range(count):
            into = pl.ds(pl.multiple_of(place_ref[at], rows), rows)
            pltpu.make_async_copy(ref.at[i], wv.at[side, into, :], sem.at[side]).start()
            at += 1
    cot_copies = []
    for side in range(2):
        copy = pltpu.make_async_copy(
            cot.at[:, pl.ds(offsets[side], half)], cv.at[side], sem.at[2 + side]
        )
        copy.start()
        cot_copies.append(copy)

    def where_is(t):
        return t // per, slice((t % per) * tile, (t % per + 1) * tile)

    def run_linear(t):
        side, cols = where_is(t)
        for m in range(0, node_count, sub):
            linear[t % 2, m : m + sub, :] = small_dot(mixed[m : m + sub, :], wv[side, :, cols])

    def run_gelu(t):
        side, cols = where_is(t)
        shift = bias[side, :, cols]
        total = jnp.zeros((8, tile), F32)
        rows = 64
        for m in range(0, node_count, rows):
            live = jnp.concatenate([alive[m : m + rows, :]] * (tile // 128), axis=1)
            value, grad = gelu_and_grad(
                linear[t % 2, m : m + rows, :] + shift, cv[side, m : m + rows, cols], live
            )
            av[side, m : m + rows, cols] = value
            lv[side, m : m + rows, cols] = grad
            total = total + jnp.sum(grad.astype(F32).reshape(rows // 8, 8, tile), axis=0)
        bias_grad[side, :, cols] = total

    def run_weight_grad(t):
        side, cols = where_is(t)
        for m in range(0, width, sub):
            part = small_dot(mixed_t[m : m + sub, :], lv[side, :, cols]).astype(BF16)
            for b in range(0, sub, block):
                into = pl.multiple_of(slot_ref[side, (m + b) // block] * block, block)
                gv[side, pl.ds(into, block), cols] = part[b : b + block]

    def all_weights(side):
        pltpu.make_async_copy(wv.at[side], wv.at[side], sem.at[side]).wait()

    outs = []
    all_weights(0)
    run_linear(0)
    for t in range(2 * per):
        if t + 1 == per:
            all_weights(1)
        if t + 1 < 2 * per:
            run_linear(t + 1)
        side = t // per
        if t % per == 0:
            cot_copies[side].wait()
        run_gelu(t)
        run_weight_grad(t)
        if (t + 1) % per == 0:
            for copy in (
                pltpu.make_async_copy(gv.at[side], (send, keep)[side], sem.at[4 + side]),
                pltpu.make_async_copy(
                    av.at[side], act.at[:, pl.ds(offsets[side], half)], sem.at[6 + side]
                ),
            ):
                copy.start()
                outs.append(copy)

    step = acc_b.shape[2]
    pending = [None, None]

    def fetch(i):
        return pltpu.make_async_copy(
            acc_in.at[:, i * step : (i + 1) * step], acc_a.at[i % 2], sem.at[8 + i % 2]
        )

    if not first:
        fetch(0).start()
    for i in range(width // step):
        if not first:
            fetch(i).wait()
            if i + 1 < width // step:
                fetch(i + 1).start()
        if pending[i % 2] is not None:
            pending[i % 2].wait()
        for m in range(0, node_count, sub):
            part = sum(
                small_dot(
                    lv[side, m : m + sub, :],
                    wv[side, i * step : (i + 1) * step, :],
                    ((1,), (1,)),
                )
                for side in range(2)
            )
            if not first:
                part = part + acc_a[i % 2, m : m + sub, :]
            if last:
                part = part * jnp.concatenate([scale[m : m + sub, :]] * (step // 128), axis=1)
            acc_b[i % 2, m : m + sub, :] = part.astype(acc_b.dtype)
        pending[i % 2] = pltpu.make_async_copy(
            acc_b.at[i % 2], acc_out.at[:, i * step : (i + 1) * step], sem.at[10 + i % 2]
        )
        pending[i % 2].start()
    for copy in pending + outs:
        if copy is not None:
            copy.wait()


def layer_chunk(start, size, last, place, slot, half, mixed, mixed_t, bias, cot, alive, scale, pieces, sides, before, block):
    node_count, width = mixed.shape
    first = before is None
    part = size // 2
    tile = min(256, part)
    step = min(256, width)
    sub = min(512, node_count)
    plan = (
        start,
        size,
        first,
        last,
        [(side, piece.shape[0], piece.shape[1]) for side, piece in zip(sides, pieces)],
        tile,
        sub,
        block,
    )
    acc_type = BF16 if last else F32
    operands = [place, slot, half, mixed, mixed_t, bias, cot, alive, scale, *pieces]
    specs = [SMEM, SMEM, SMEM, VMEM, VMEM, VMEM, ANY, VMEM, VMEM] + [ANY] * len(pieces)
    aliases = {}
    if not first:
        operands += list(before)
        specs += [ANY, ANY]
        aliases = {len(operands) - 1: 0}
    return pl.pallas_call(
        functools.partial(layer_kernel, plan),
        in_specs=specs,
        out_specs=[ANY, ANY, ANY, VMEM, ANY],
        out_shape=[
            jax.ShapeDtypeStruct((node_count, width), BF16),
            jax.ShapeDtypeStruct((width, part), BF16),
            jax.ShapeDtypeStruct((width, part), BF16),
            jax.ShapeDtypeStruct((2, 8, part), F32),
            jax.ShapeDtypeStruct((node_count, width), acc_type),
        ],
        scratch_shapes=[
            pltpu.VMEM((2, width, part), BF16),
            pltpu.VMEM((2, node_count, part), BF16),
            pltpu.VMEM((2, node_count, part), BF16),
            pltpu.VMEM((2, node_count, part), BF16),
            pltpu.VMEM((2, width, part), BF16),
            pltpu.VMEM((2, node_count, tile), F32),
            pltpu.VMEM((2, node_count, step), F32),
            pltpu.VMEM((2, node_count, step), acc_type),
            pltpu.SemaphoreType.DMA((12,)),
        ],
        input_output_aliases=aliases,
        compiler_params=pltpu.CompilerParams(vmem_limit_bytes=32 * MIB),
        name="layer_chunk",
    )(*operands)


def rim_grad_kernel(sizes, cnt_t_ref, grad_ref, *outs):
    node_count = grad_ref.shape[0]
    part = small_dot(cnt_t_ref[node_count:, :], grad_ref[...])
    at = 0
    for out, rows in zip(outs, sizes):
        out[...] = part[at : at + rows].astype(BF16)
        at += rows


def rim_grads(cnt_t, grad, sizes):
    micro, table, node_count = cnt_t.shape
    width = grad.shape[1]
    wide = min(512, width)
    return pl.pallas_call(
        functools.partial(rim_grad_kernel, sizes),
        grid=(micro, width // wide),
        in_specs=[
            pl.BlockSpec((None, table, node_count), lambda m, j: (m, 0, 0)),
            pl.BlockSpec((node_count, wide), lambda m, j: (m, j)),
        ],
        out_specs=[pl.BlockSpec((None, rows, wide), lambda m, j: (m, 0, j)) for rows in sizes],
        out_shape=[jax.ShapeDtypeStruct((micro, rows, width), BF16) for rows in sizes],
        compiler_params=pltpu.CompilerParams(vmem_limit_bytes=24 * MIB),
        name="rim_grads",
    )(cnt_t, grad)


def own_grad_kernel(cnt_t_ref, grad_ref, out_ref, head_ref):
    part = small_dot(cnt_t_ref[...], grad_ref[...])
    out_ref[...] = part.astype(BF16)
    head_ref[...] = part[: head_ref.shape[0]]


def own_grads(cnt_t, grad, rim_size):
    micro, _, node_count = cnt_t.shape
    width = grad.shape[1]
    wide = min(512, width)
    return pl.pallas_call(
        own_grad_kernel,
        grid=(micro, width // wide),
        in_specs=[
            pl.BlockSpec((None, node_count, node_count), lambda m, j: (m, 0, 0)),
            pl.BlockSpec((node_count, wide), lambda m, j: (m, j)),
        ],
        out_specs=[
            pl.BlockSpec((None, node_count, wide), lambda m, j: (m, 0, j)),
            pl.BlockSpec((None, rim_size, wide), lambda m, j: (m, 0, j)),
        ],
        out_shape=[
            jax.ShapeDtypeStruct((micro, node_count, width), BF16),
            jax.ShapeDtypeStruct((micro, rim_size, width), F32),
        ],
        compiler_params=pltpu.CompilerParams(vmem_limit_bytes=24 * MIB),
        name="own_grads",
    )(cnt_t, grad)


class Layout:
    def __init__(self, blks, shards):
        self.blks, self.shards = blks, shards
        self.tuned = shards == 2 and blks % 4 == 0
        self.sizes = {"z": blks // 4, "y": 2, "c": 2, "x": shards}

    def number(self, at):
        return ((at["z"] * 2 + at["y"]) * 2 + at["c"]) * self.shards + at["x"]

    def here(self):
        blk, shard = lax.axis_index("blk"), lax.axis_index("shard")
        return {"z": blk // 4, "y": blk // 2 % 2, "c": blk % 2, "x": shard}

    def spots(self):
        for z in range(self.sizes["z"]):
            for y in range(2):
                for c in range(2):
                    for x in range(self.shards):
                        yield {"z": z, "y": y, "c": c, "x": x}

    def shift(self, value, axes, by):
        pairs = []
        for spot in self.spots():
            axis = axes[spot["c"]]
            there = dict(spot)
            there[axis] = (spot[axis] + by) % self.sizes[axis]
            pairs.append((self.number(spot), self.number(there)))
        return lax.ppermute(value, BOTH, pairs)

    def swap(self, value):
        return self.shift(value, "cc", 1)


def from_shard(value, by):
    count = lax.axis_size("shard")
    return lax.ppermute(value, "shard", [(i, (i + by) % count) for i in range(count)])


def near_swap(value):
    count = lax.axis_size("blk")
    return lax.ppermute(value, "blk", [(i, i ^ 1) for i in range(count)])


def far_swap(value):
    count = lax.axis_size("blk")
    return lax.ppermute(value, "blk", [(i, (i + (1 if i % 2 else -1)) % count) for i in range(count)])


def gather_phases(layout, base, orders):
    steps = len(orders[0])
    current = base
    for step in range(steps):
        axes = (orders[0][step], orders[1][step])
        count = layout.sizes[axes[0]]
        got = [current] + [layout.shift(current, axes, k) for k in range(1, count)]
        if step == steps - 1:
            return got
        current = jnp.concatenate(got, axis=0)
    return [current]


def gathered_from(layout, order, bases):
    current = [{"c": b} for b in range(bases)]
    for axis in order:
        current = [dict(entry, **{axis: k}) for k in range(layout.sizes[axis]) for entry in current]
    return current


def gathered_numbers(layout, orders, bases, here, swapped):
    core = here["c"] ^ 1 if swapped else here["c"]
    tables = []
    for order in orders:
        entries = gathered_from(layout, order, bases)
        tables.append({axis: np.array([e[axis] for e in entries], np.int32) for axis in "zycx"})
    back = {axis: jnp.where(core == 0, tables[0][axis], tables[1][axis]) for axis in "zycx"}
    at = {axis: (here[axis] - back[axis]) % layout.sizes[axis] for axis in "zyx"}
    at["c"] = core ^ back["c"]
    return layout.number(at)


def slots_of(layout, orders, here, swapped):
    core = here["c"] ^ 1 if swapped else here["c"]
    number = np.arange(layout.blks * layout.shards)
    at = {
        "x": number % layout.shards,
        "c": number // layout.shards % 2,
        "y": number // layout.shards // 2 % 2,
        "z": number // layout.shards // 4,
    }
    results = []
    for order in orders:
        slot = 0
        for axis in order:
            count = layout.sizes[axis]
            ahead = (at[axis] - here[axis]) % count
            slot = slot * count + (ahead - 1) % count
        results.append(slot * 2 + (at["c"] ^ core))
    return jnp.where(core == 0, results[0], results[1]).astype(jnp.int32)


def reduce_phases(layout, parts, orders, kind):
    for step in range(len(orders[0])):
        axes = (orders[0][step], orders[1][step])
        count = layout.sizes[axes[0]]
        size = parts[0].shape[0] // count
        got = []
        for k in range(1, count):
            total = sum(part[(k - 1) * size : k * size].astype(F32) for part in parts)
            got.append(layout.shift(total.astype(kind), axes, k))
        parts = [part[(count - 1) * size :] for part in parts] + got
    return sum(part.astype(F32) for part in parts)


def per_device(layout, features, weight, bias, cotangent, neighbours, live_count):
    micro_count, node_count, width = features.shape
    shards = layout.shards
    devices = layout.blks * shards
    rim = node_count // 8
    own_rows = weight.shape[0]
    here = layout.here()
    core = here["c"]
    tuned = layout.tuned and own_rows % 16 == 0
    chunks = []
    at = 0
    for share in CHUNKS:
        chunks.append((at, int(width * share)))
        at += int(width * share)

    rim_own = features[:, :rim]
    rim_cross = [from_shard(rim_own, shards - k) for k in range(1, shards)]
    rim_far = far_swap(rim_own)

    if tuned:
        halves = [
            jnp.concatenate([weight[:, s + h * n // 2 : s + (h + 1) * n // 2] for s, n in chunks], axis=1)
            for h in range(2)
        ]
        ours = jnp.where(core == 0, halves[0], halves[1])
        theirs = layout.swap(jnp.where(core == 0, halves[1], halves[0]))
        base = jnp.stack([ours, theirs])

    rim_near = near_swap(jnp.concatenate([rim_own] + rim_cross, axis=1))
    rim_far_cross = [from_shard(rim_far, shards - k) for k in range(1, shards)]
    pieces = rim_cross + [rim_near, rim_far] + rim_far_cross
    table = node_count + sum(piece.shape[1] for piece in pieces)

    span = shards * rim
    shifted = neighbours - node_count
    section = shifted // span
    ahead = (shifted // rim % shards - here["x"]) % shards
    near_section = jnp.where(core == 0, 2, 1)
    base_slot = jnp.where(
        section == 0,
        node_count - rim,
        jnp.where(section == near_section, node_count + span - rim, node_count + 2 * span - rim),
    )
    slot = base_slot + ahead * rim + shifted % rim
    slot = jnp.where((section == 0) & (ahead == 0), shifted % rim, slot)
    codes = jnp.where(neighbours < node_count, neighbours, slot)
    degree = jnp.sum((neighbours >= 0).astype(F32), axis=2)
    alive = (jnp.arange(node_count, dtype=jnp.int32)[None, :] < live_count).astype(F32)
    weighting = alive / (degree + 1.0)
    total_nodes = micro_count * node_count
    alive_wide = jnp.broadcast_to(alive.reshape(total_nodes, 1), (total_nodes, 128))
    scale_wide = jnp.broadcast_to(weighting.reshape(total_nodes, 1), (total_nodes, 128))
    cnt, cnt_t = count_tables(codes, table)
    mixed, mixed_t = mix(cnt, scale_wide, features, pieces)

    if tuned:
        order = GATHER_ORDER[0]
        tiny = jnp.broadcast_to(jnp.pad(bias, (0, 128 - own_rows))[None, None, :], (1, 8, 128))
        tiny = jnp.concatenate([tiny, layout.swap(tiny)], axis=0)
        tiny = jnp.concatenate(gather_phases(layout, tiny, order), axis=0)[:, 0, :own_rows]
        owner = gathered_numbers(layout, order, 2, here, False)
        pick = (owner[None, :] == jnp.arange(devices)[:, None]).astype(F32)
        bias_full = jnp.dot(pick, tiny.astype(F32), precision=lax.Precision.HIGHEST).reshape(width)
    else:
        bias_full = lax.all_gather(bias, BOTH, axis=0, tiled=True).astype(F32)

    cot_rows = cotangent.reshape(total_nodes, width)
    before = None
    weight_grads = []
    bias_parts = []
    half_at = 0
    for j, (start, size) in enumerate(chunks):
        part = size // 2
        if tuned:
            order = GATHER_ORDER[j]
            mine = gather_phases(layout, base[:, :, half_at : half_at + part], order)
            other = [layout.swap(piece) for piece in mine]
            chunk_pieces = other + mine
            sides = [0] * len(other) + [1] * len(mine)
            place = jnp.concatenate(
                [gathered_numbers(layout, order, 2, here, flag) for flag in (True, False)]
            ) * own_rows
            slot_table = jnp.stack(
                [slots_of(layout, REDUCE_ORDER[j], here, flag) for flag in (True, False)]
            )
            block = own_rows
        else:
            whole = lax.all_gather(weight[:, start : start + size], BOTH, axis=0, tiled=True)
            low_half, high_half = whole[:, :part], whole[:, part:]
            chunk_pieces = [
                jnp.where(core == 0, high_half, low_half)[None],
                jnp.where(core == 0, low_half, high_half)[None],
            ]
            sides = [0, 1]
            place = jnp.zeros((2,), jnp.int32)
            block = 64
            slot_table = jnp.broadcast_to(jnp.arange(width // block, dtype=jnp.int32), (2, width // block))
        half_at += part
        pair = bias_full[start : start + size].reshape(2, 1, part)
        pair = jnp.where(core == 0, pair[::-1], pair)
        act, send, keep, bias_rows, acc = layer_chunk(
            start,
            size,
            j == len(chunks) - 1,
            place.astype(jnp.int32),
            slot_table.astype(jnp.int32),
            core.astype(jnp.int32).reshape(1),
            mixed,
            mixed_t,
            pair,
            cot_rows,
            alive_wide,
            scale_wide,
            chunk_pieces,
            sides,
            before,
            block,
        )
        before = (acc, act)
        bias_row = jnp.sum(bias_rows, axis=1)
        bias_parts.append(jnp.where(core == 0, bias_row[::-1], bias_row).reshape(size))
        if tuned:
            send = send.reshape(devices, own_rows, part)
            keep = keep.reshape(devices, own_rows, part)
            both = reduce_phases(layout, [keep, layout.swap(send)], REDUCE_ORDER[j], BF16)
            ours, theirs = both[0], layout.swap(both[1])
        else:
            ours = lax.psum_scatter(
                jnp.where(core == 0, keep, send), BOTH, scatter_dimension=0, tiled=True
            ).astype(F32)
            theirs = lax.psum_scatter(
                jnp.where(core == 0, send, keep), BOTH, scatter_dimension=0, tiled=True
            ).astype(F32)
        if tuned:
            low_half = jnp.where(core == 0, ours, theirs)
            high_half = jnp.where(core == 0, theirs, ours)
        else:
            low_half, high_half = ours, theirs
        weight_grads += [low_half, high_half]

    grad = acc
    sizes = [rim] * (shards - 1) + [span] + [rim] * shards
    parts = rim_grads(cnt_t, grad, sizes)
    cross, near, far = parts[: shards - 1], parts[shards - 1], parts[shards:]
    local, head = own_grads(cnt_t, grad, rim)
    near_back = near_swap(near).astype(F32)
    own_sum = near_back[:, :rim]
    far_sum = far[0].astype(F32)
    for k in range(1, shards):
        both = jnp.concatenate(
            [
                (cross[k - 1].astype(F32) + near_back[:, k * rim : (k + 1) * rim]).astype(BF16),
                far[k],
            ],
            axis=1,
        )
        both = from_shard(both, k).astype(F32)
        own_sum = own_sum + both[:, :rim]
        far_sum = far_sum + both[:, rim:]
    far_back = far_swap(far_sum.astype(BF16)).astype(F32)
    head = (head + own_sum + far_back).astype(BF16)
    feature_grad = lax.dynamic_update_slice(local, head, (0, 0, 0))

    bias_sum = jnp.concatenate(bias_parts)
    if tuned:
        order = REDUCE_ORDER[0]
        slot_table = slots_of(layout, order, here, False)
        pick = (slot_table[None, :] == jnp.arange(devices)[:, None]).astype(F32)
        tiny = jnp.dot(pick, bias_sum.reshape(devices, own_rows), precision=lax.Precision.HIGHEST)
        tiny = jnp.broadcast_to(
            jnp.pad(tiny, ((0, 0), (0, 128 - own_rows)))[:, None, :], (devices, 8, 128)
        )
        both = reduce_phases(layout, [tiny], order, F32)
        bias_out = (both[0] + layout.swap(both[1]))[0, :own_rows]
    else:
        bias_out = lax.psum_scatter(bias_sum, BOTH, scatter_dimension=0, tiled=True)

    return (
        before[1].reshape(features.shape),
        feature_grad,
        jnp.concatenate(weight_grads, axis=1),
        bias_out,
    )


def solution(mesh):
    layout = Layout(mesh.shape["blk"], mesh.shape["shard"])
    rows = P(None, BOTH, None)
    return jax.shard_map(
        functools.partial(per_device, layout),
        mesh=mesh,
        in_specs=(rows, P(BOTH, None), P(BOTH), rows, rows, P(None, BOTH)),
        out_specs=(rows, rows, P(BOTH, None), P(BOTH)),
        check_vma=False,
    )
```

time: 617 us -> 286 us (0.46); the launches traced: 607 us -> 286 us
  waiting for transfers between devices: 304 us -> 106 us
  matrix products: 110 us -> 0.25 us
  blocking collectives: 106 us -> 0 us
  Pallas kernels: 0 us -> 78.9 us
  starting transfers between devices: 13.4 us -> 61.1 us
  other arithmetic: 43.1 us -> 9.68 us
  between operations: 14.3 us -> 1.3 us
  local copies, waits for them, and re-layouts: 16.3 us -> 28.3 us
    reduce_scatter x3 -> x0, waiting for transfers between devices: 303 us -> none  [the longest x1 303 us: reduce_grads(): lax.psum_scatter(weight_term, ('blk', 'shard'), scatter_dimension=0, tile...]
    dot_general x10 -> x2, matrix products: 110 us -> 0.25 us  [the longest x1 0.13 us: per_device(): jnp.dot(pick, bias_sum.reshape(devices, own_rows), precision=lax.Precisio...]
    ppermute x8 -> x48, waiting for transfers between devices: 0.02 us -> 106 us  [the longest x41 85.3 us: shift(): return lax.ppermute(value, BOTH, pairs)]
    unnamed x2 -> x0, blocking collectives: 86.6 us -> none
    pallas_call x0 -> x6, Pallas kernels: none -> 78.9 us  [the longest x2 47.4 us: layer_chunk(): pl.pallas_call(functools.partial(layer_kernel, plan), in_specs=specs, out...]
    ppermute x8 -> x48, starting transfers between devices: 13.2 us -> 61.1 us  [the longest x41 55.9 us: shift(): return lax.ppermute(value, BOTH, pairs)]
    unnamed x25 -> x56, local copies, waits for them, and re-layouts: 2.26 us -> 21.7 us
    all_gather x2 -> x0, blocking collectives: 19.2 us -> none  [per_device(): group_rims = lax.all_gather(rim_rows, 'shard', axis=0, tiled=True)]
  transfers between devices with their start and end apart: 12 -> 48, of which waited for: 1 -> 17; matrix products, arithmetic and copies ran while one was open for 20% -> 6% of each run, Pallas kernels for 0% -> 19%
where the time goes in v1:
time: 286 us
  waiting for transfers between devices  106 us (37%)
  Pallas kernels  78.9 us (28%)
  starting transfers between devices  61.1 us (21%)
  local copies, waits for them, and re-layouts  28.3 us (10%)
  other arithmetic  9.68 us (3%)
    ppermute x41, waiting for transfers between devices, shift(): return lax.ppermute(value, BOTH, pairs)  85.3 us
    ppermute x41, starting transfers between devices, shift(): return lax.ppermute(value, BOTH, pairs)  55.9 us
    pallas_call x2, Pallas kernels, layer_chunk(): pl.pallas_call(functools.partial(layer_kernel, plan), in_specs=specs, out...  47.4 us
    unnamed x56, local copies, waits for them, and re-layouts  21.7 us
    ppermute x3, waiting for transfers between devices, from_shard(): lax.ppermute(value, 'shard', [(i, (i + by) % count) for i in range(count)])  20.7 us
    pallas_call x1, Pallas kernels, count_tables(): pl.pallas_call(functools.partial(count_kernel, node_count), grid=(micro,)...  14.1 us
    pallas_call x1, Pallas kernels, mix(): pl.pallas_call(mix_kernel, grid=(micro, width // wide), in_specs=[pl.Bloc...  8.45 us
  transfers between devices with their start and end apart: 48, of which 17 were waited for; matrix products, arithmetic and copies ran while one was open for 6% of the time, Pallas kernels for 19%

profile of v1, /device:TPU:0, one launch (start us, length us, event | category | flops | bytes accessed | tf_op | source)
XLA Modules:
  0.0 285.6 jit_solution(4920281494616597440)
XLA Ops:
  6.6 5.0 %collective-permute-start.13 = (bf16[2,64,512]{2,1,0:T(8,128)(2,1)S(1)}, bf16[2,64,512]{2,1,0:T(8,128)(2,1)S(1)}, u32[]{:S(2)}, u32[]{:S(2)}) collective-permute-start(bf16[2,64,512]{2,1,0:T(8,128)(2,1)S(1)} %get-tuple-element.73), channel_id=1, source_target_pairs={{0,24},{1,25},{2,26},{3,27},{4,28},{5,29},{6,30},{7,31},{8,0},{9,1... | collective-permute-start | bytes 393224 | tf_op jit(solution)/shard_map/ppermute | solution.py:406
  13.7 2.9 %collective-permute-start.20 = (bf16[2,64,512]{2,1,0:T(8,128)(2,1)S(1)}, bf16[2,64,512]{2,1,0:T(8,128)(2,1)S(1)}, u32[]{:S(2)}, u32[]{:S(2)}) collective-permute-start(bf16[2,64,512]{2,1,0:T(8,128)(2,1)S(1)} %get-tuple-element.45), channel_id=1, source_target_pairs={{0,24},{1,25},{2,26},{3,27},{4,28},{5,29},{6,30},{7,31},{8,0},{9,1... | collective-permute-start | bytes 393224 | tf_op jit(solution)/shard_map/ppermute | solution.py:406
  17.7 6.9 %collective-permute-done.12 = bf16[2,64,512]{2,1,0:T(8,128)(2,1)S(1)} collective-permute-done((bf16[2,64,512]{2,1,0:T(8,128)(2,1)S(1)}, bf16[2,64,512]{2,1,0:T(8,128)(2,1)S(1)}, u32[]{:S(2)}, u32[]{:S(2)}) %collective-permute-start.12) | collective-permute-done | bytes 131104 | tf_op jit(solution)/shard_map/ppermute | solution.py:406
  26.2 2.2 collective-permute-start.7
  28.4 6.1 %collective-permute-done.19 = bf16[2,64,512]{2,1,0:T(8,128)(2,1)S(1)} collective-permute-done((bf16[2,64,512]{2,1,0:T(8,128)(2,1)S(1)}, bf16[2,64,512]{2,1,0:T(8,128)(2,1)S(1)}, u32[]{:S(2)}, u32[]{:S(2)}) %collective-permute-start.19) | collective-permute-done | bytes 131104 | tf_op jit(solution)/shard_map/ppermute | solution.py:406
  40.7 9.9 %collective-permute-done.21 = bf16[8,64,512]{2,1,0:T(8,128)(2,1)S(1)} collective-permute-done((bf16[8,64,512]{2,1,0:T(8,128)(2,1)S(1)}, bf16[8,64,512]{2,1,0:T(8,128)(2,1)S(1)}, u32[]{:S(2)}, u32[]{:S(2)}) %collective-permute-start.21) | collective-permute-done | bytes 524320 | tf_op jit(solution)/shard_map/ppermute | solution.py:406
  51.5 5.8 %collective-permute-start.23 = (bf16[16,64,512]{2,1,0:T(8,128)(2,1)}, bf16[16,64,512]{2,1,0:T(8,128)(2,1)}, u32[]{:S(2)}, u32[]{:S(2)}) collective-permute-start(bf16[16,64,512]{2,1,0:T(8,128)(2,1)} %constant_dynamic-update-slice_fusion.5.refs_11_), channel_id=1, source_target_pairs={{0,4},{1,5},{2,3},{3,2},{4,0},{5,1},{6,7},{7,6},{8,12},{9,13},{10,... | collective-permute-start | bytes 3145736 | tf_op jit(solution)/shard_map/ppermute | solution.py:406
  59.5 3.2 %collective-permute-done.6 = bf16[2,8,128]{2,0,1:T(2,128)(2,1)S(1)} collective-permute-done((bf16[2,8,128]{2,0,1:T(2,128)(2,1)S(1)}, bf16[2,8,128]{2,0,1:T(2,128)(2,1)S(1)}, u32[]{:S(2)}, u32[]{:S(2)}) %collective-permute-start.6) | collective-permute-done | bytes 4128 | tf_op jit(solution)/shard_map/ppermute | solution.py:406
  64.3 3.9 %collective-permute-done.5 = bf16[2,8,128]{2,0,1:T(2,128)(2,1)S(1)} collective-permute-done((bf16[2,8,128]{2,0,1:T(2,128)(2,1)S(1)}, bf16[2,8,128]{2,0,1:T(2,128)(2,1)S(1)}, u32[]{:S(2)}, u32[]{:S(2)}) %collective-permute-start.5) | collective-permute-done | bytes 4128 | tf_op jit(solution)/shard_map/ppermute | solution.py:406
  69.8 8.2 %collective-permute-done.8 = bf16[8,8,128]{2,0,1:T(8,128)(2,1)S(1)} collective-permute-done((bf16[8,8,128]{2,0,1:T(8,128)(2,1)S(1)}, bf16[8,8,128]{2,0,1:T(8,128)(2,1)S(1)}, u32[]{:S(2)}, u32[]{:S(2)}) %collective-permute-start.8) | collective-permute-done | bytes 16416 | tf_op jit(solution)/shard_map/ppermute | solution.py:406
  78.0 2.1 collective-permute-start.9
  82.0 8.6 %collective-permute-start.22 = (bf16[16,64,512]{2,1,0:T(8,128)(2,1)}, bf16[16,64,512]{2,1,0:T(8,128)(2,1)}, u32[]{:S(2)}, u32[]{:S(2)}) collective-permute-start(bf16[16,64,512]{2,1,0:T(8,128)(2,1)} %constant_dynamic-update-slice_fusion.5.refs_11_), channel_id=1, source_target_pairs={{0,2},{1,3},{2,0},{3,1},{4,6},{5,7},{6,4},{7,5},{8,10},{9,11},{10,... | collective-permute-start | bytes 3145736 | tf_op jit(solution)/shard_map/ppermute | solution.py:406
  91.5 14.1 %count_tables.1 = (bf16[2,512,832]{2,1,0:T(8,128)(2,1)S(1)}, bf16[2,832,512]{2,1,0:T(8,128)(2,1)S(1)}) custom-call(s32[2,512,16]{2,1,0:T(8,128)S(1)} %copy.72.code_ref, s32[2,16,512]{2,1,0:T(8,128)S(1)} %fusion.93.code_t_ref), custom_call_target="tpu_custom_call" | custom-call | tf_op jit(solution)/shard_map/count_tables/pallas_call | solution.py:62
  107.5 2.2 copy-done.5
  112.2 8.4 %mix.1 = (bf16[1024,2048]{1,0:T(8,128)(2,1)S(1)}, bf16[2048,1024]{1,0:T(8,128)(2,1)S(1)}) custom-call(bf16[2,512,832]{2,1,0:T(8,128)(2,1)S(1)} %copy-done.11, f32[1024,128]{1,0:T(8,128)S(1)} %broadcast_in_dim.52.scale_ref.refs_8_, bf16[2,512,2048]{2,1,0:T(8,128)(2,1)S(1)} %copy-done.5, bf16[2,64,2048]{2,1,0:T(8,128)(2,1)S(1)} %collective-permute-done.refs_0_, ...), custom_call_target="tpu_custom_call" | custom-call | tf_op jit(solution)/shard_map/mix/pallas_call | solution.py:105
  120.9 22.5 %layer_chunk.2 = (bf16[1024,2048]{1,0:T(8,128)(2,1)}, bf16[2048,512]{1,0:T(8,128)(2,1)S(1)}, bf16[2048,512]{1,0:T(8,128)(2,1)S(1)}, f32[2,8,512]{2,1,0:T(8,128)S(1)}, f32[1024,2048]{1,0:T(8,128)}) custom-call(s32[64]{0:T(128)S(1)} %add_multiply_fusion.refs_0_, s32[2,32]{1,0:T(2,128)S(1)} %pad_add_fusion.refs_1_, s32[1]{0:T(128)} %bitcast.2.refs_2_, ...), custom_call_target="tpu_custom_call" | custom-call | tf_op jit(solution)/shard_map/layer_chunk/pallas_call | solution.py:294
  146.2 2.2 copy-done.4
  148.4 24.9 %layer_chunk.3 = (bf16[1024,2048]{1,0:T(8,128)(2,1)}, bf16[2048,512]{1,0:T(8,128)(2,1)S(1)}, bf16[2048,512]{1,0:T(8,128)(2,1)S(1)}, f32[2,8,512]{2,1,0:T(8,128)S(1)}, bf16[1024,2048]{1,0:T(8,128)(2,1)S(1)}) custom-call(s32[64]{0:T(128)S(1)} %add_multiply_fusion.refs_0_, s32[2,32]{1,0:T(2,128)S(1)} %pad_add_fusion.refs_1_, ...), custom_call_target="tpu_custom_call", output_to_operand_aliasing={{0}: (14, {})} | custom-call | tf_op jit(solution)/shard_map/layer_chunk/pallas_call | solution.py:294
  173.3 2.0 copy-done
  180.9 2.1 collective-permute-done.42
  182.9 2.0 collective-permute-start.43
  185.0 2.2 copy-done.1
  187.2 3.3 %rim_grads.1 = (bf16[2,64,2048]{2,1,0:T(8,128)(2,1)S(1)}, bf16[2,128,2048]{2,1,0:T(8,128)(2,1)S(1)}, bf16[2,64,2048]{2,1,0:T(8,128)(2,1)S(1)}, bf16[2,64,2048]{2,1,0:T(8,128)(2,1)S(1)}) custom-call(bf16[2,832,512]{2,1,0:T(8,128)(2,1)S(1)} %get-tuple-element.30.cnt_t_ref, bf16[1024,2048]{1,0:T(8,128)(2,1)S(1)} %copy-done.1), custom_call_target="tpu_custom_call" | custom-call | tf_op jit(solution)/shard_map/rim_grads/pallas_call | solution.py:335
  191.2 3.8 %collective-permute-start.46 = (f32[2,8,128]{2,1,0:T(8,128)S(1)}, f32[2,8,128]{2,1,0:T(8,128)S(1)}, u32[]{:S(2)}, u32[]{:S(2)}) collective-permute-start(f32[2,8,128]{2,1,0:T(8,128)S(1)} %get-tuple-element.83), channel_id=1, source_target_pairs={{0,24},{1,25},{2,26},{3,27},{4,28},{5,29},{6,30},{7,31},{8,0},{9,1... | collective-permute-start | bytes 24584 | tf_op jit(solution)/shard_map/ppermute | solution.py:406
  196.9 5.6 %own_grads.1 = (bf16[2,512,2048]{2,1,0:T(8,128)(2,1)}, f32[2,64,2048]{2,1,0:T(8,128)S(1)}) custom-call(bf16[2,832,512]{2,1,0:T(8,128)(2,1)S(1)} %get-tuple-element.30.cnt_t_ref, bf16[1024,2048]{1,0:T(8,128)(2,1)S(1)} %copy-done.1), custom_call_target="tpu_custom_call" | custom-call | tf_op jit(solution)/shard_map/own_grads/pallas_call | solution.py:359
  208.0 20.7 %collective-permute-done.26 = bf16[2,128,2048]{2,1,0:T(8,128)(2,1)S(1)} collective-permute-done((bf16[2,128,2048]{2,1,0:T(8,128)(2,1)S(1)}, bf16[2,128,2048]{2,1,0:T(8,128)(2,1)S(1)}, u32[]{:S(2)}, u32[]{:S(2)}) %collective-permute-start.26) | collective-permute-done | bytes 1048608 | tf_op jit(solution)/shard_map/ppermute | solution.py:414
  229.1 18.1 %collective-permute-done.36 = bf16[16,64,512]{2,1,0:T(8,128)(2,1)S(1)} collective-permute-done((bf16[16,64,512]{2,1,0:T(8,128)(2,1)S(1)}, bf16[16,64,512]{2,1,0:T(8,128)(2,1)S(1)}, u32[]{:S(2)}, u32[]{:S(2)}) %collective-permute-start.36) | collective-permute-done | bytes 1048608 | tf_op jit(solution)/shard_map/ppermute | solution.py:406
  247.6 14.8 %collective-permute-done.29 = bf16[16,64,512]{2,1,0:T(8,128)(2,1)S(1)} collective-permute-done((bf16[16,64,512]{2,1,0:T(8,128)(2,1)S(1)}, bf16[16,64,512]{2,1,0:T(8,128)(2,1)S(1)}, u32[]{:S(2)}, u32[]{:S(2)}) %collective-permute-start.29) | collective-permute-done | bytes 1048608 | tf_op jit(solution)/shard_map/ppermute | solution.py:406
  264.7 3.6 %collective-permute-start.40 = (bf16[2,64,512]{2,1,0:T(8,128)(2,1)S(1)}, bf16[2,64,512]{2,1,0:T(8,128)(2,1)S(1)}, u32[]{:S(2)}, u32[]{:S(2)}) collective-permute-start(bf16[2,64,512]{2,1,0:T(8,128)(2,1)S(1)} %get-tuple-element.58), channel_id=1, source_target_pairs={{0,24},{1,25},{2,26},{3,27},{4,28},{5,29},{6,30},{7,31},{8,0},{9,1... | collective-permute-start | bytes 393224 | tf_op jit(solution)/shard_map/ppermute | solution.py:406
  269.4 2.4 collective-permute-done.30
  272.4 3.5 %collective-permute-start.33 = (bf16[2,64,512]{2,1,0:T(8,128)(2,1)S(1)}, bf16[2,64,512]{2,1,0:T(8,128)(2,1)S(1)}, u32[]{:S(2)}, u32[]{:S(2)}) collective-permute-start(bf16[2,64,512]{2,1,0:T(8,128)(2,1)S(1)} %get-tuple-element.55), channel_id=1, source_target_pairs={{0,24},{1,25},{2,26},{3,27},{4,28},{5,29},{6,30},{7,31},{8,0},{9,1... | collective-permute-start | bytes 393224 | tf_op jit(solution)/shard_map/ppermute | solution.py:406
  280.0 3.2 %collective-permute-done.32 = bf16[2,64,512]{2,1,0:T(8,128)(2,1)S(1)} collective-permute-done((bf16[2,64,512]{2,1,0:T(8,128)(2,1)S(1)}, bf16[2,64,512]{2,1,0:T(8,128)(2,1)S(1)}, u32[]{:S(2)}, u32[]{:S(2)}) %collective-permute-start.32) | collective-permute-done | bytes 131104 | tf_op jit(solution)/shard_map/ppermute | solution.py:406
  (205 shorter events, 57.6 us)
Async XLA Ops:
  1.3 15.3 %collective-permute-start.4 = (bf16[1,8,128]{2,0,1:T(2,128)(2,1)S(1)}, bf16[1,8,128]{2,0,1:T(2,128)(2,1)S(1)}, u32[]{:S(2)}, u32[]{:S(2)}) collective-permute-start(bf16[1,8,128]{2,0,1:T(2,128)(2,1)S(1)} %broadcast_in_dim.53), channel_id=1, source_target_pairs={{0,2},{1,3},{2,0},{3,1},{4,6},{5,7},{6,4},{7,5},{8,10},{9,11},{10,... | collective-permute-start | bytes 6152 | tf_op jit(solution)/shard_map/ppermute | solution.py:406
  6.6 11.1 %collective-permute-start.13 = (bf16[2,64,512]{2,1,0:T(8,128)(2,1)S(1)}, bf16[2,64,512]{2,1,0:T(8,128)(2,1)S(1)}, u32[]{:S(2)}, u32[]{:S(2)}) collective-permute-start(bf16[2,64,512]{2,1,0:T(8,128)(2,1)S(1)} %get-tuple-element.73), channel_id=1, source_target_pairs={{0,24},{1,25},{2,26},{3,27},{4,28},{5,29},{6,30},{7,31},{8,0},{9,1... | collective-permute-start | bytes 393224 | tf_op jit(solution)/shard_map/ppermute | solution.py:406
  11.6 13.0 %collective-permute-start.12 = (bf16[2,64,512]{2,1,0:T(8,128)(2,1)S(1)}, bf16[2,64,512]{2,1,0:T(8,128)(2,1)S(1)}, u32[]{:S(2)}, u32[]{:S(2)}) collective-permute-start(bf16[2,64,512]{2,1,0:T(8,128)(2,1)S(1)} %get-tuple-element.73), channel_id=1, source_target_pairs={{0,16},{1,17},{2,18},{3,19},{4,20},{5,21},{6,22},{7,23},{8,24},{9,... | collective-permute-start | bytes 393224 | tf_op jit(solution)/shard_map/ppermute | solution.py:406
  11.6 13.0 %collective-permute-start.11 = (bf16[2,64,512]{2,1,0:T(8,128)(2,1)S(1)}, bf16[2,64,512]{2,1,0:T(8,128)(2,1)S(1)}, u32[]{:S(2)}, u32[]{:S(2)}) collective-permute-start(bf16[2,64,512]{2,1,0:T(8,128)(2,1)S(1)} %get-tuple-element.73), channel_id=1, source_target_pairs={{0,8},{1,9},{2,10},{3,11},{4,12},{5,13},{6,14},{7,15},{8,16},{9,17... | collective-permute-start | bytes 393224 | tf_op jit(solution)/shard_map/ppermute | solution.py:406
  13.7 12.5 %collective-permute-start.20 = (bf16[2,64,512]{2,1,0:T(8,128)(2,1)S(1)}, bf16[2,64,512]{2,1,0:T(8,128)(2,1)S(1)}, u32[]{:S(2)}, u32[]{:S(2)}) collective-permute-start(bf16[2,64,512]{2,1,0:T(8,128)(2,1)S(1)} %get-tuple-element.45), channel_id=1, source_target_pairs={{0,24},{1,25},{2,26},{3,27},{4,28},{5,29},{6,30},{7,31},{8,0},{9,1... | collective-permute-start | bytes 393224 | tf_op jit(solution)/shard_map/ppermute | solution.py:406
  16.6 17.9 %collective-permute-start.19 = (bf16[2,64,512]{2,1,0:T(8,128)(2,1)S(1)}, bf16[2,64,512]{2,1,0:T(8,128)(2,1)S(1)}, u32[]{:S(2)}, u32[]{:S(2)}) collective-permute-start(bf16[2,64,512]{2,1,0:T(8,128)(2,1)S(1)} %get-tuple-element.45), channel_id=1, source_target_pairs={{0,16},{1,17},{2,18},{3,19},{4,20},{5,21},{6,22},{7,23},{8,24},{9,... | collective-permute-start | bytes 393224 | tf_op jit(solution)/shard_map/ppermute | solution.py:406
  17.7 18.3 %collective-permute-start.18 = (bf16[2,64,512]{2,1,0:T(8,128)(2,1)S(1)}, bf16[2,64,512]{2,1,0:T(8,128)(2,1)S(1)}, u32[]{:S(2)}, u32[]{:S(2)}) collective-permute-start(bf16[2,64,512]{2,1,0:T(8,128)(2,1)S(1)} %get-tuple-element.45), channel_id=1, source_target_pairs={{0,8},{1,9},{2,10},{3,11},{4,12},{5,13},{6,14},{7,15},{8,16},{9,17... | collective-permute-start | bytes 393224 | tf_op jit(solution)/shard_map/ppermute | solution.py:406
  24.6 38.1 %collective-permute-start.2 = (bf16[2,64,2048]{2,1,0:T(8,128)(2,1)S(1)}, bf16[2,64,2048]{2,1,0:T(8,128)(2,1)S(1)}, u32[]{:S(2)}, u32[]{:S(2)}) collective-permute-start(bf16[2,64,2048]{2,1,0:T(8,128)(2,1)S(1)} %slice.319), channel_id=1, source_target_pairs={{0,30},{2,4},{4,2},{6,8},{8,6},{10,12},{12,10},{14,16},{16,14},{18... | collective-permute-start | bytes 1572872 | tf_op jit(solution)/shard_map/ppermute | solution.py:424
  24.6 55.5 %collective-permute-start = (bf16[2,64,2048]{2,1,0:T(8,128)(2,1)S(1)}, bf16[2,64,2048]{2,1,0:T(8,128)(2,1)S(1)}, u32[]{:S(2)}, u32[]{:S(2)}) collective-permute-start(bf16[2,64,2048]{2,1,0:T(8,128)(2,1)S(1)} %slice.319), channel_id=1, source_target_pairs={{0,1},{1,0},{2,3},{3,2},{4,5},{5,4},{6,7},{7,6},{8,9},{9,8},{10,11... | collective-permute-start | bytes 1572872 | tf_op jit(solution)/shard_map/ppermute | solution.py:414
  26.2 32.0 %collective-permute-start.7 = (bf16[2,8,128]{2,0,1:T(2,128)(2,1)S(1)}, bf16[2,8,128]{2,0,1:T(2,128)(2,1)S(1)}, u32[]{:S(2)}, u32[]{:S(2)}) collective-permute-start(bf16[2,8,128]{2,0,1:T(2,128)(2,1)S(1)} %pad_maximum_fusion.6), channel_id=1, source_target_pairs={{0,24},{1,25},{2,26},{3,27},{4,28},{5,29},{6,30},{7,31},{8,0},{9,1... | collective-permute-start | bytes 12296 | tf_op jit(solution)/shard_map/ppermute | solution.py:406
  34.5 22.8 %collective-permute-start.14 = (bf16[8,64,512]{2,1,0:T(8,128)(2,1)S(1)}, bf16[8,64,512]{2,1,0:T(8,128)(2,1)S(1)}, u32[]{:S(2)}, u32[]{:S(2)}) collective-permute-start(bf16[8,64,512]{2,1,0:T(8,128)(2,1)S(1)} %pad_maximum_fusion.2), channel_id=1, source_target_pairs={{0,1},{1,0},{2,6},{3,7},{4,5},{5,4},{6,2},{7,3},{8,9},{9,8},{10,14... | collective-permute-start | bytes 1572872 | tf_op jit(solution)/shard_map/ppermute | solution.py:406
  36.2 14.5 %collective-permute-start.21 = (bf16[8,64,512]{2,1,0:T(8,128)(2,1)S(1)}, bf16[8,64,512]{2,1,0:T(8,128)(2,1)S(1)}, u32[]{:S(2)}, u32[]{:S(2)}) collective-permute-start(bf16[8,64,512]{2,1,0:T(8,128)(2,1)S(1)} %pad_maximum_fusion.3), channel_id=1, source_target_pairs={{0,1},{1,0},{2,6},{3,7},{4,5},{5,4},{6,2},{7,3},{8,9},{9,8},{10,14... | collective-permute-start | bytes 1572872 | tf_op jit(solution)/shard_map/ppermute | solution.py:406
  51.5 39.2 %collective-permute-start.23 = (bf16[16,64,512]{2,1,0:T(8,128)(2,1)}, bf16[16,64,512]{2,1,0:T(8,128)(2,1)}, u32[]{:S(2)}, u32[]{:S(2)}) collective-permute-start(bf16[16,64,512]{2,1,0:T(8,128)(2,1)} %constant_dynamic-update-slice_fusion.5.refs_11_), channel_id=1, source_target_pairs={{0,4},{1,5},{2,3},{3,2},{4,0},{5,1},{6,7},{7,6},{8,12},{9,13},{10,... | collective-permute-start | bytes 3145736 | tf_op jit(solution)/shard_map/ppermute | solution.py:406
  58.1 33.1 %collective-permute-start.16 = (bf16[16,64,512]{2,1,0:T(8,128)(2,1)}, bf16[16,64,512]{2,1,0:T(8,128)(2,1)}, u32[]{:S(2)}, u32[]{:S(2)}) collective-permute-start(bf16[16,64,512]{2,1,0:T(8,128)(2,1)} %constant_dynamic-update-slice_fusion.refs_11_), channel_id=1, source_target_pairs={{0,4},{1,5},{2,3},{3,2},{4,0},{5,1},{6,7},{7,6},{8,12},{9,13},{10,... | collective-permute-start | bytes 3145736 | tf_op jit(solution)/shard_map/ppermute | solution.py:406
  62.7 27.9 %collective-permute-start.3 = (bf16[2,64,2048]{2,1,0:T(8,128)(2,1)S(1)}, bf16[2,64,2048]{2,1,0:T(8,128)(2,1)S(1)}, u32[]{:S(2)}, u32[]{:S(2)}) collective-permute-start(bf16[2,64,2048]{2,1,0:T(8,128)(2,1)S(1)} %collective-permute-done.2.refs_2_), channel_id=1, source_target_pairs={{0,1},{1,0},{2,3},{3,2},{4,5},{5,4},{6,7},{7,6},{8,9},{9,8},{10,11... | collective-permute-start | bytes 1572872 | tf_op jit(solution)/shard_map/ppermute | solution.py:414
  68.2 9.8 %collective-permute-start.8 = (bf16[8,8,128]{2,0,1:T(8,128)(2,1)S(1)}, bf16[8,8,128]{2,0,1:T(8,128)(2,1)S(1)}, u32[]{:S(2)}, u32[]{:S(2)}) collective-permute-start(bf16[8,8,128]{2,0,1:T(8,128)(2,1)S(1)} %concatenate.87), channel_id=1, source_target_pairs={{0,1},{1,0},{2,6},{3,7},{4,5},{5,4},{6,2},{7,3},{8,9},{9,8},{10,14... | collective-permute-start | bytes 49160 | tf_op jit(solution)/shard_map/ppermute | solution.py:406
  81.1 26.1 %collective-permute-start.1 = (bf16[2,128,2048]{2,1,0:T(8,128)(2,1)}, bf16[2,128,2048]{2,1,0:T(8,128)(2,1)}, u32[]{:S(2)}, u32[]{:S(2)}) collective-permute-start(bf16[2,128,2048]{2,1,0:T(8,128)(2,1)} %pad_maximum_fusion), channel_id=1, source_target_pairs={{0,2},{2,0},{4,6},{6,4},{8,10},{10,8},{12,14},{14,12},{16,18},{18,... | collective-permute-start | bytes 3145736 | tf_op jit(solution)/shard_map/ppermute | solution.py:419
  82.0 38.7 %collective-permute-start.22 = (bf16[16,64,512]{2,1,0:T(8,128)(2,1)}, bf16[16,64,512]{2,1,0:T(8,128)(2,1)}, u32[]{:S(2)}, u32[]{:S(2)}) collective-permute-start(bf16[16,64,512]{2,1,0:T(8,128)(2,1)} %constant_dynamic-update-slice_fusion.5.refs_11_), channel_id=1, source_target_pairs={{0,2},{1,3},{2,0},{3,1},{4,6},{5,7},{6,4},{7,5},{8,10},{9,11},{10,... | collective-permute-start | bytes 3145736 | tf_op jit(solution)/shard_map/ppermute | solution.py:406
  90.6 55.5 %collective-permute-start.15 = (bf16[16,64,512]{2,1,0:T(8,128)(2,1)}, bf16[16,64,512]{2,1,0:T(8,128)(2,1)}, u32[]{:S(2)}, u32[]{:S(2)}) collective-permute-start(bf16[16,64,512]{2,1,0:T(8,128)(2,1)} %constant_dynamic-update-slice_fusion.refs_11_), channel_id=1, source_target_pairs={{0,2},{1,3},{2,0},{3,1},{4,6},{5,7},{6,4},{7,5},{8,10},{9,11},{10,... | collective-permute-start | bytes 3145736 | tf_op jit(solution)/shard_map/ppermute | solution.py:406
  90.7 30.0 %collective-permute-start.24 = (bf16[16,64,512]{2,1,0:T(8,128)(2,1)}, bf16[16,64,512]{2,1,0:T(8,128)(2,1)}, u32[]{:S(2)}, u32[]{:S(2)}) collective-permute-start(bf16[16,64,512]{2,1,0:T(8,128)(2,1)} %collective-permute-done.23.refs_12_), channel_id=1, source_target_pairs={{0,2},{1,3},{2,0},{3,1},{4,6},{5,7},{6,4},{7,5},{8,10},{9,11},{10,... | collective-permute-start | bytes 3145736 | tf_op jit(solution)/shard_map/ppermute | solution.py:406
  91.2 55.0 %collective-permute-start.17 = (bf16[16,64,512]{2,1,0:T(8,128)(2,1)}, bf16[16,64,512]{2,1,0:T(8,128)(2,1)}, u32[]{:S(2)}, u32[]{:S(2)}) collective-permute-start(bf16[16,64,512]{2,1,0:T(8,128)(2,1)} %collective-permute-done.16.refs_12_), channel_id=1, source_target_pairs={{0,2},{1,3},{2,0},{3,1},{4,6},{5,7},{6,4},{7,5},{8,10},{9,11},{10,... | collective-permute-start | bytes 3145736 | tf_op jit(solution)/shard_map/ppermute | solution.py:406
  180.2 24.5 %collective-permute-start.35 = (bf16[32,64,512]{2,1,0:T(8,128)(2,1)}, bf16[32,64,512]{2,1,0:T(8,128)(2,1)S(1)}, u32[]{:S(2)}, u32[]{:S(2)}) collective-permute-start(bf16[32,64,512]{2,1,0:T(8,128)(2,1)} %bitcast.80), channel_id=1, source_target_pairs={{0,2},{1,3},{2,0},{3,1},{4,6},{5,7},{6,4},{7,5},{8,10},{9,11},{10,... | collective-permute-start | bytes 6291464 | tf_op jit(solution)/shard_map/ppermute | solution.py:406
  185.0 20.6 %collective-permute-start.28 = (bf16[32,64,512]{2,1,0:T(8,128)(2,1)}, bf16[32,64,512]{2,1,0:T(8,128)(2,1)S(1)}, u32[]{:S(2)}, u32[]{:S(2)}) collective-permute-start(bf16[32,64,512]{2,1,0:T(8,128)(2,1)} %bitcast.79), channel_id=1, source_target_pairs={{0,2},{1,3},{2,0},{3,1},{4,6},{5,7},{6,4},{7,5},{8,10},{9,11},{10,... | collective-permute-start | bytes 6291464 | tf_op jit(solution)/shard_map/ppermute | solution.py:406
  190.5 12.1 %collective-permute-start.25 = (bf16[2,128,2048]{2,1,0:T(8,128)(2,1)S(1)}, bf16[2,128,2048]{2,1,0:T(8,128)(2,1)S(1)}, u32[]{:S(2)}, u32[]{:S(2)}) collective-permute-start(bf16[2,128,2048]{2,1,0:T(8,128)(2,1)S(1)} %get-tuple-element.34), channel_id=1, source_target_pairs={{0,2},{2,0},{4,6},{6,4},{8,10},{10,8},{12,14},{14,12},{16,18},{18,... | collective-permute-start | bytes 3145736 | tf_op jit(solution)/shard_map/ppermute | solution.py:419
  191.2 11.3 %collective-permute-start.46 = (f32[2,8,128]{2,1,0:T(8,128)S(1)}, f32[2,8,128]{2,1,0:T(8,128)S(1)}, u32[]{:S(2)}, u32[]{:S(2)}) collective-permute-start(f32[2,8,128]{2,1,0:T(8,128)S(1)} %get-tuple-element.83), channel_id=1, source_target_pairs={{0,24},{1,25},{2,26},{3,27},{4,28},{5,29},{6,30},{7,31},{8,0},{9,1... | collective-permute-start | bytes 24584 | tf_op jit(solution)/shard_map/ppermute | solution.py:406
  203.1 25.6 %collective-permute-start.26 = (bf16[2,128,2048]{2,1,0:T(8,128)(2,1)S(1)}, bf16[2,128,2048]{2,1,0:T(8,128)(2,1)S(1)}, u32[]{:S(2)}, u32[]{:S(2)}) collective-permute-start(bf16[2,128,2048]{2,1,0:T(8,128)(2,1)S(1)} %pad_maximum_fusion.1), channel_id=1, source_target_pairs={{0,1},{1,0},{2,3},{3,2},{4,5},{5,4},{6,7},{7,6},{8,9},{9,8},{10,11... | collective-permute-start | bytes 3145736 | tf_op jit(solution)/shard_map/ppermute | solution.py:414
  205.0 42.3 %collective-permute-start.36 = (bf16[16,64,512]{2,1,0:T(8,128)(2,1)S(1)}, bf16[16,64,512]{2,1,0:T(8,128)(2,1)S(1)}, u32[]{:S(2)}, u32[]{:S(2)}) collective-permute-start(bf16[16,64,512]{2,1,0:T(8,128)(2,1)S(1)} %fusion), channel_id=1, source_target_pairs={{0,1},{1,0},{2,6},{3,7},{4,5},{5,4},{6,2},{7,3},{8,9},{9,8},{10,14... | collective-permute-start | bytes 3145736 | tf_op jit(solution)/shard_map/ppermute | solution.py:406
  205.9 56.5 %collective-permute-start.29 = (bf16[16,64,512]{2,1,0:T(8,128)(2,1)S(1)}, bf16[16,64,512]{2,1,0:T(8,128)(2,1)S(1)}, u32[]{:S(2)}, u32[]{:S(2)}) collective-permute-start(bf16[16,64,512]{2,1,0:T(8,128)(2,1)S(1)} %fusion.1), channel_id=1, source_target_pairs={{0,1},{1,0},{2,6},{3,7},{4,5},{5,4},{6,2},{7,3},{8,9},{9,8},{10,14... | collective-permute-start | bytes 3145736 | tf_op jit(solution)/shard_map/ppermute | solution.py:406
  229.1 34.0 %collective-permute-start.27 = (bf16[2,64,2048]{2,1,0:T(8,128)(2,1)S(1)}, bf16[2,64,2048]{2,1,0:T(8,128)(2,1)S(1)}, u32[]{:S(2)}, u32[]{:S(2)}) collective-permute-start(bf16[2,64,2048]{2,1,0:T(8,128)(2,1)S(1)} %fusion.2), channel_id=1, source_target_pairs={{0,30},{2,4},{4,2},{6,8},{8,6},{10,12},{12,10},{14,16},{16,14},{18... | collective-permute-start | bytes 1572872 | tf_op jit(solution)/shard_map/ppermute | solution.py:424
  247.5 16.7 %collective-permute-start.37 = (bf16[8,64,512]{2,1,0:T(8,128)(2,1)S(1)}, bf16[8,64,512]{2,1,0:T(8,128)(2,1)S(1)}, u32[]{:S(2)}, u32[]{:S(2)}) collective-permute-start(bf16[8,64,512]{2,1,0:T(8,128)(2,1)S(1)} %fusion.8), channel_id=1, source_target_pairs={{0,4},{1,5},{2,3},{3,2},{4,0},{5,1},{6,7},{7,6},{8,12},{9,13},{10,... | collective-permute-start | bytes 1572872 | tf_op jit(solution)/shard_map/ppermute | solution.py:406
  264.4 11.5 %collective-permute-start.38 = (bf16[2,64,512]{2,1,0:T(8,128)(2,1)S(1)}, bf16[2,64,512]{2,1,0:T(8,128)(2,1)S(1)}, u32[]{:S(2)}, u32[]{:S(2)}) collective-permute-start(bf16[2,64,512]{2,1,0:T(8,128)(2,1)S(1)} %get-tuple-element.57), channel_id=1, source_target_pairs={{0,8},{1,9},{2,10},{3,11},{4,12},{5,13},{6,14},{7,15},{8,16},{9,17... | collective-permute-start | bytes 393224 | tf_op jit(solution)/shard_map/ppermute | solution.py:406
  264.7 12.4 %collective-permute-start.40 = (bf16[2,64,512]{2,1,0:T(8,128)(2,1)S(1)}, bf16[2,64,512]{2,1,0:T(8,128)(2,1)S(1)}, u32[]{:S(2)}, u32[]{:S(2)}) collective-permute-start(bf16[2,64,512]{2,1,0:T(8,128)(2,1)S(1)} %get-tuple-element.58), channel_id=1, source_target_pairs={{0,24},{1,25},{2,26},{3,27},{4,28},{5,29},{6,30},{7,31},{8,0},{9,1... | collective-permute-start | bytes 393224 | tf_op jit(solution)/shard_map/ppermute | solution.py:406
  (40 other events, 356.3 us)

commit v2 on v1

v2 whole, which is shorter than its diff:
```python
import functools

import jax
import jax.numpy as jnp
import numpy as np
from jax import lax
from jax.experimental import pallas as pl
from jax.experimental.pallas import tpu as pltpu
from jax.sharding import PartitionSpec as P

BOTH = ("blk", "shard")
F32 = jnp.float32
BF16 = jnp.bfloat16
MIB = 1 << 20
GELU_A = 0.7978845608028654
GELU_B = 0.044715
HBM = pl.BlockSpec(memory_space=pltpu.HBM)
VMEM = pl.BlockSpec(memory_space=pltpu.VMEM)
SMEM = pl.BlockSpec(memory_space=pltpu.SMEM)

CHUNKS = (0.5, 0.5)
GATHER_ORDER = ("hlxy", "hlyx")
REDUCE_ORDER = (("xylh", "yxlh"), ("xylh", "yxlh"))


def cost(us):
    return pl.CostEstimate(flops=int(us * 1.1e9), bytes_accessed=0, transcendentals=0)


def held(array, space):
    return pltpu.with_memory_space_constraint(array, space)


def small_dot(a, b, contract=((1,), (0,))):
    return lax.dot_general(a, b, (contract, ((), ())), preferred_element_type=F32)


def count_kernel(code_ref, cnt_ref, cnt_t_ref):
    node_count, slots = code_ref.shape
    table = cnt_ref.shape[1]
    step = 64
    kind = jnp.int16

    def some_nodes(i, carry):
        at = pl.ds(pl.multiple_of(i * step, step), step)
        codes = code_ref[at, :].astype(kind)
        column = lax.broadcasted_iota(kind, (step, table), 1)
        row = lax.broadcasted_iota(kind, (step, table), 0) + (i * step).astype(kind)
        total = jnp.where(column == row, BF16(2), BF16(0))
        for k in range(slots):
            total = total + jnp.where(column == codes[:, k : k + 1], BF16(1), BF16(0))
        cnt_ref[at, :] = total
        return carry

    lax.fori_loop(0, node_count // step, some_nodes, 0)
    cnt_t_ref[...] = cnt_ref[...].T


def count_tables(codes, table):
    micro, node_count, slots = codes.shape
    return pl.pallas_call(
        count_kernel,
        grid=(micro,),
        in_specs=[pl.BlockSpec((None, node_count, slots), lambda m: (m, 0, 0))],
        out_specs=[
            pl.BlockSpec((None, node_count, table), lambda m: (m, 0, 0)),
            pl.BlockSpec((None, table, node_count), lambda m: (m, 0, 0)),
        ],
        out_shape=[
            jax.ShapeDtypeStruct((micro, node_count, table), BF16),
            jax.ShapeDtypeStruct((micro, table, node_count), BF16),
        ],
        compiler_params=pltpu.CompilerParams(vmem_limit_bytes=24 * MIB),
        cost_estimate=cost(6),
        name="count_tables",
    )(codes)


def mix_kernel(counts, cnt_ref, scale_ref, own_ref, *refs):
    piece_refs, (mixed_ref, mixed_t_ref, token_ref, rim) = refs[:-4], refs[-4:]
    node_count = own_ref.shape[0]
    for micro, count in enumerate(counts):
        first = sum(counts[:micro])

        @pl.when(pl.program_id(0) == micro)
        def _():
            at = 0
            for piece in piece_refs[first : first + count]:
                rim[at : at + piece.shape[0], :] = piece[...]
                at += piece.shape[0]

    total = small_dot(cnt_ref[:, :node_count], own_ref[...])
    total = total + small_dot(cnt_ref[:, node_count:], rim[...])
    scale = jnp.concatenate([scale_ref[...]] * (total.shape[1] // 128), axis=1)
    low = (total * scale).astype(BF16)
    mixed_ref[...] = low
    mixed_t_ref[...] = low.T
    token_ref[...] = jnp.zeros_like(token_ref)


def mix(cnt, scale, features, pieces):
    micro, node_count, width = features.shape
    table = cnt.shape[2]
    wide = min(512, width)

    def rows_of(piece, which):
        return pl.BlockSpec(
            (piece.shape[0], wide), lambda m, j: (0, jnp.where(m == which, j, (micro - 1 - m) * 0))
        )

    return pl.pallas_call(
        functools.partial(mix_kernel, [len(group) for group in pieces]),
        grid=(micro, width // wide),
        in_specs=[
            pl.BlockSpec((None, node_count, table), lambda m, j: (m, 0, 0)),
            pl.BlockSpec((node_count, 128), lambda m, j: (m, 0)),
            pl.BlockSpec((None, node_count, wide), lambda m, j: (m, 0, j)),
        ]
        + [rows_of(piece, which) for which in range(micro) for piece in pieces[which]],
        out_specs=[
            pl.BlockSpec((node_count, wide), lambda m, j: (m, j)),
            pl.BlockSpec((wide, node_count), lambda m, j: (j, m)),
            pl.BlockSpec((8, 128), lambda m, j: (0, 0)),
        ],
        out_shape=[
            pltpu.VMEM((micro * node_count, width), BF16),
            pltpu.VMEM((width, micro * node_count), BF16),
            jax.ShapeDtypeStruct((8, 128), F32),
        ],
        scratch_shapes=[pltpu.VMEM((table - node_count, wide), BF16)],
        compiler_params=pltpu.CompilerParams(vmem_limit_bytes=24 * MIB),
        cost_estimate=cost(6),
        name="mix",
    )(cnt, scale, features, *[piece for group in pieces for piece in group])


def gelu_and_grad(linear, incoming, alive):
    square = linear * linear
    bend = jnp.tanh(linear * (GELU_A + (GELU_A * GELU_B) * square))
    share = 0.5 + 0.5 * bend
    value = linear * share
    slope = share + value * (1.0 - bend) * (GELU_A + (3.0 * GELU_A * GELU_B) * square)
    return (value * alive).astype(BF16), (incoming.astype(F32) * alive * slope).astype(BF16)


def half_kernel(plan, *refs):
    start, half, side, first, tail, keeps, whole, blocks, bias_blocks, inner, rows, tile, sub, block = plan
    refs = list(refs)
    place_ref, chip_ref, slot_ref, half_ref, _, mixed, mixed_t, cot, alive = refs[:9]
    del refs[:9]
    n_pieces = 1 if whole else len(blocks)
    pieces = refs[:n_pieces]
    del refs[:n_pieces]
    bias_pieces = refs[: len(bias_blocks)]
    del refs[: len(bias_blocks)]
    bias = None if bias_blocks else refs.pop(0)
    bias_sums_in = None
    if not first:
        bias_sums_in = refs[0]
        del refs[:2]
    act, out, bias_sums, grad_out, wv = refs[:5]
    del refs[:5]
    bias_out = refs.pop(0) if bias_blocks else None
    cv, av, gv, linear, bias_raw, sem = refs
    node_count, width = mixed.shape
    tiles = half // tile
    mine = half_ref[0]
    holder = mine if side else 1 - mine
    offset = pl.multiple_of(start + holder * half, 128)

    def columns(t):
        return slice(t * tile, (t + 1) * tile)

    for t in range(tiles):
        at = 0
        if whole:
            part = pl.ds(pl.multiple_of(holder * half + t * tile, 128), tile)
            pltpu.make_async_copy(pieces[0].at[:, part], wv.at[:, columns(t)], sem.at[t]).start()
        for ref, count in zip(pieces, blocks):
            for i in range(count):
                for k in range(inner):
                    into = pl.ds(pl.multiple_of(place_ref[side, at], rows), rows)
                    pltpu.make_async_copy(
                        ref.at[i, k * rows : (k + 1) * rows, columns(t)],
                        wv.at[into, columns(t)],
                        sem.at[t],
                    ).start()
                    at += 1
        if t == 0:
            seen = 0
            for ref, count in zip(bias_pieces, bias_blocks):
                for i in range(count):
                    pltpu.make_async_copy(
                        ref.at[i, inner * rows : inner * rows + 16, 0:128],
                        bias_raw.at[chip_ref[seen]],
                        sem.at[tiles + 2],
                    ).start()
                    seen += 1
            cot_copy = pltpu.make_async_copy(cot.at[:, pl.ds(offset, half)], cv, sem.at[tiles])
            cot_copy.start()

    if first:
        bias_sums[...] = jnp.zeros_like(bias_sums)
    else:
        bias_sums[...] = bias_sums_in[...]
    if bias_blocks:
        pltpu.make_async_copy(bias_raw, bias_raw, sem.at[tiles + 2]).wait()
        for chip in range(bias_raw.shape[0] // 2):
            pair = bias_raw[2 * chip].astype(F32) + bias_raw[2 * chip + 1].astype(F32)
            bias_out[2 * chip] = jnp.where(mine == 0, pair[:8], pair[8:])
            bias_out[2 * chip + 1] = jnp.where(mine == 0, pair[8:], pair[:8])
        bias = bias_out

    def run_linear(t):
        pltpu.make_async_copy(wv.at[:, columns(t)], wv.at[:, columns(t)], sem.at[t]).wait()
        for m in range(0, node_count, sub):
            linear[t % 2, m : m + sub, :] = small_dot(mixed[m : m + sub, :], wv[:, columns(t)])

    def run_gelu(t):
        group = offset // 128 + t * (tile // 128)
        shift = jnp.concatenate([bias[group + k] for k in range(tile // 128)], axis=1)[:1]
        total = jnp.zeros((8, tile), F32)
        step = 64
        for m in range(0, node_count, step):
            live = jnp.concatenate([alive[m : m + step, :]] * (tile // 128), axis=1)
            value, grad = gelu_and_grad(
                linear[t % 2, m : m + step, :] + shift, cv[m : m + step, columns(t)], live
            )
            av[m : m + step, columns(t)] = value
            grad_out[m : m + step, columns(t)] = grad
            total = total + jnp.sum(grad.astype(F32).reshape(step // 8, 8, tile), axis=0)
        for k in range(tile // 128):
            bias_sums[group + k] = total[:, k * 128 : (k + 1) * 128]

    def run_weight_grad(t):
        for m in range(0, width, sub):
            part = small_dot(mixed_t[m : m + sub, :], grad_out[:, columns(t)]).astype(BF16)
            for b in range(0, sub, block):
                into = pl.multiple_of(slot_ref[side, (m + b) // block], 16)
                gv[pl.ds(into, block), columns(t)] = part[b : b + block]

    run_linear(0)
    cot_copy.wait()
    for t in range(tiles):
        if t + 1 < tiles:
            run_linear(t + 1)
        run_gelu(t)
        run_weight_grad(t)
    act_copy = pltpu.make_async_copy(av, act.at[:, pl.ds(offset, half)], sem.at[tiles + 1])
    act_copy.start()
    if tail:
        for pair in range(width // block // 2):
            chip = pair // 2
            base = slot_ref[side, chip * 4 + pair % 2] - holder * block
            if keeps:
                both = jnp.concatenate(
                    [bias_sums[2 * chip + holder], bias_sums[2 * chip + 1 - holder]], axis=0
                )
                both = jnp.concatenate([both, jnp.zeros((16, half - 128), F32)], axis=1)
            else:
                both = jnp.zeros((16, half), F32)
            gv[pl.ds(pl.multiple_of(base + 2 * block, 16), 16), :] = both.astype(BF16)
    out_copy = pltpu.make_async_copy(gv, out, sem.at[tiles])
    out_copy.start()
    act_copy.wait()
    out_copy.wait()


def layer_half(
    start, half, side, tail, tables, token, mixed, mixed_t, bias, cot, alive, pieces, bias_pieces, rows, before, block
):
    node_count, width = mixed.shape
    first = before is None
    tile = min(256, half)
    sub = min(512, node_count)
    groups = width // 128
    out_rows = width + 16 * (width // block // 2) if tail else width
    plan = (
        start,
        half,
        side,
        first,
        tail,
        tail and side == 1,
        pieces[0].ndim == 2,
        [piece.shape[0] for piece in pieces if piece.ndim == 3],
        [piece.shape[0] for piece in bias_pieces],
        2,
        rows,
        tile,
        sub,
        block,
    )
    operands = [*tables, token]
    operands += [held(array, pltpu.VMEM) for array in (mixed, mixed_t)]
    operands += [held(cot, pltpu.HBM), alive]
    operands += [held(array, pltpu.HBM) for array in (*pieces, *bias_pieces)]
    specs = [SMEM] * 4 + [HBM, VMEM, VMEM, HBM, VMEM] + [HBM] * (len(pieces) + len(bias_pieces))
    if not bias_pieces:
        operands.append(bias)
        specs.append(VMEM)
    aliases = {}
    if not first:
        operands += list(before)
        specs += [VMEM, HBM]
        aliases = {len(operands) - 1: 0}
    out_specs = [HBM, HBM, VMEM, VMEM, VMEM]
    out_shape = [
        pltpu.HBM((node_count, width), BF16),
        pltpu.HBM((out_rows, half), BF16),
        jax.ShapeDtypeStruct((groups, 8, 128), F32),
        pltpu.VMEM((node_count, half), BF16),
        pltpu.VMEM((width, half), BF16),
    ]
    if bias_pieces:
        out_specs.append(VMEM)
        out_shape.append(jax.ShapeDtypeStruct((groups, 8, 128), F32))
    return pl.pallas_call(
        functools.partial(half_kernel, plan),
        in_specs=specs,
        out_specs=out_specs,
        out_shape=out_shape,
        scratch_shapes=[
            pltpu.VMEM((node_count, half), BF16),
            pltpu.VMEM((node_count, half), BF16),
            pltpu.VMEM((out_rows, half), BF16),
            pltpu.VMEM((2, node_count, tile), F32),
            pltpu.VMEM((groups, 16, 128), BF16),
            pltpu.SemaphoreType.DMA((half // tile + 3,)),
        ],
        input_output_aliases=aliases,
        compiler_params=pltpu.CompilerParams(vmem_limit_bytes=16 * MIB),
        cost_estimate=cost(8),
        name="layer_half",
    )(*operands)


def mixed_grad_kernel(count, scale, *refs):
    grads, weights, out = refs[:count], refs[count : 2 * count], refs[2 * count]
    node_count, width = out.shape
    tile = min(256, width)
    sub = min(512, node_count)
    for d in range(0, width, tile):
        for m in range(0, node_count, sub):
            part = sum(
                small_dot(grad[m : m + sub, :], weight[d : d + tile, :], ((1,), (1,)))
                for grad, weight in zip(grads, weights)
            )
            part = part * jnp.concatenate([scale[m : m + sub, :]] * (tile // 128), axis=1)
            out[m : m + sub, d : d + tile] = part.astype(BF16)


def mixed_grad(scale, grads, weights):
    node_count, width = grads[0].shape[0], weights[0].shape[0]
    return pl.pallas_call(
        functools.partial(mixed_grad_kernel, len(grads)),
        in_specs=[VMEM] * (1 + 2 * len(grads)),
        out_specs=VMEM,
        out_shape=jax.ShapeDtypeStruct((node_count, width), BF16),
        compiler_params=pltpu.CompilerParams(vmem_limit_bytes=16 * MIB),
        cost_estimate=cost(10),
        name="mixed_grad",
    )(scale, *[held(array, pltpu.VMEM) for array in (*grads, *weights)])


def rim_grad_kernel(sizes, cnt_t_ref, grad_ref, *outs):
    node_count = grad_ref.shape[0]
    part = small_dot(cnt_t_ref[node_count:, :], grad_ref[...])
    at = 0
    for out, rows in zip(outs, sizes):
        out[...] = part[at : at + rows].astype(BF16)
        at += rows


def rim_grads(cnt_t, grad, sizes):
    micro, table, node_count = cnt_t.shape
    width = grad.shape[1]
    wide = min(512, width)
    return pl.pallas_call(
        functools.partial(rim_grad_kernel, sizes),
        grid=(micro, width // wide),
        in_specs=[
            pl.BlockSpec((None, table, node_count), lambda m, j: (m, 0, 0)),
            pl.BlockSpec((node_count, wide), lambda m, j: (m, j)),
        ],
        out_specs=[pl.BlockSpec((None, rows, wide), lambda m, j: (m, 0, j)) for rows in sizes],
        out_shape=[jax.ShapeDtypeStruct((micro, rows, width), BF16) for rows in sizes],
        compiler_params=pltpu.CompilerParams(vmem_limit_bytes=24 * MIB),
        cost_estimate=cost(3),
        name="rim_grads",
    )(cnt_t, grad)


def own_grad_kernel(cnt_t_ref, grad_ref, out_ref, head_ref):
    part = small_dot(cnt_t_ref[...], grad_ref[...])
    out_ref[...] = part.astype(BF16)
    head_ref[...] = part[: head_ref.shape[0]]


def own_grads(cnt_t, grad, rim_size):
    micro, _, node_count = cnt_t.shape
    width = grad.shape[1]
    wide = min(512, width)
    return pl.pallas_call(
        own_grad_kernel,
        grid=(micro, width // wide),
        in_specs=[
            pl.BlockSpec((None, node_count, node_count), lambda m, j: (m, 0, 0)),
            pl.BlockSpec((node_count, wide), lambda m, j: (m, j)),
        ],
        out_specs=[
            pl.BlockSpec((None, node_count, wide), lambda m, j: (m, 0, j)),
            pl.BlockSpec((None, rim_size, wide), lambda m, j: (m, 0, j)),
        ],
        out_shape=[
            jax.ShapeDtypeStruct((micro, node_count, width), BF16),
            jax.ShapeDtypeStruct((micro, rim_size, width), F32),
        ],
        compiler_params=pltpu.CompilerParams(vmem_limit_bytes=24 * MIB),
        cost_estimate=cost(4),
        name="own_grads",
    )(cnt_t, grad)


class Layout:
    def __init__(self, blks, shards):
        self.blks, self.shards = blks, shards
        self.tuned = shards == 2 and blks == 16
        self.sizes = {"h": blks // 8, "l": 2, "y": 2, "c": 2, "x": shards}

    def number(self, at):
        blk = ((at["h"] * 2 + at["l"]) * 2 + at["y"]) * 2 + at["c"]
        return blk * self.shards + at["x"]

    def place(self, blk, shard):
        return {"h": blk // 8, "l": blk // 4 % 2, "y": blk // 2 % 2, "c": blk % 2, "x": shard}

    def here(self):
        return self.place(lax.axis_index("blk"), lax.axis_index("shard"))

    def spots(self):
        for number in range(self.blks * self.shards):
            yield self.place(number // self.shards, number % self.shards)

    def shift(self, value, axes, by):
        pairs = []
        for spot in self.spots():
            axis = axes[spot["c"]]
            there = dict(spot)
            there[axis] = (spot[axis] + by) % self.sizes[axis]
            pairs.append((self.number(spot), self.number(there)))
        return lax.ppermute(value, BOTH, pairs)

    def swap(self, value):
        return self.shift(value, "cc", 1)


def from_shard(value, by):
    count = lax.axis_size("shard")
    return lax.ppermute(value, "shard", [(i, (i + by) % count) for i in range(count)])


def near_swap(value):
    count = lax.axis_size("blk")
    return lax.ppermute(value, "blk", [(i, i ^ 1) for i in range(count)])


def far_swap(value):
    count = lax.axis_size("blk")
    return lax.ppermute(value, "blk", [(i, (i + (1 if i % 2 else -1)) % count) for i in range(count)])


def tie(value, *others):
    return lax.optimization_barrier((value, others))[0]


def gather_step(layout, current, orders, step):
    axes = (orders[0][step], orders[1][step])
    return [current] + [
        layout.shift(current, axes, k) for k in range(1, layout.sizes[axes[0]])
    ]


def reduce_step(layout, parts, orders, step):
    size = parts[0].shape[0] // layout.sizes[orders[0][step]]
    return [
        sum(part[k * size : (k + 1) * size].astype(F32) for part in parts).astype(BF16)
        for k in range(layout.sizes[orders[0][step]] - 1)
    ]


def reduce_send(layout, parts, sums, orders, step):
    axes = (orders[0][step], orders[1][step])
    got = [layout.shift(total, axes, k + 1) for k, total in enumerate(sums)]
    return [part[part.shape[0] - sums[0].shape[0] :] for part in parts] + got


def gathered_from(layout, order, bases):
    current = [{"c": b} for b in range(bases)]
    for axis in order:
        current = [dict(entry, **{axis: k}) for k in range(layout.sizes[axis]) for entry in current]
    return current


def gathered_numbers(layout, orders, bases, here, swapped):
    core = here["c"] ^ 1 if swapped else here["c"]
    tables = []
    for order in orders:
        entries = gathered_from(layout, order, bases)
        tables.append({axis: np.array([e[axis] for e in entries], np.int32) for axis in "hlycx"})
    back = {axis: jnp.where(core == 0, tables[0][axis], tables[1][axis]) for axis in "hlycx"}
    at = {axis: (here[axis] - back[axis]) % layout.sizes[axis] for axis in "hlyx"}
    at["c"] = core ^ back["c"]
    return layout.number(at)


def slots_of(layout, orders, here, swapped):
    core = here["c"] ^ 1 if swapped else here["c"]
    number = np.arange(layout.blks * layout.shards)
    at = layout.place(number // layout.shards, number % layout.shards)
    results = []
    for order in orders:
        slot = 0
        for axis in order:
            count = layout.sizes[axis]
            ahead = (at[axis] - here[axis]) % count
            slot = slot * count + (ahead - 1) % count
        results.append(slot * 2 + (at["c"] ^ core))
    return jnp.where(core == 0, results[0], results[1]).astype(jnp.int32)


def per_device(layout, features, weight, bias, cotangent, neighbours, live_count):
    micro_count, node_count, width = features.shape
    shards = layout.shards
    devices = layout.blks * shards
    rim = node_count // 8
    span = shards * rim
    own_rows = weight.shape[0]
    here = layout.here()
    core = here["c"]
    tuned = layout.tuned and own_rows * shards == 128
    chunks = []
    at = 0
    for share in CHUNKS:
        chunks.append((at, int(width * share)))
        at += int(width * share)
    back_a, back_b = REDUCE_ORDER

    rim_own = [features[m, :rim] for m in range(2)]
    far_0 = [far_swap(rim_own[0])]
    cross_1 = [from_shard(rim_own[1], shards - k) for k in range(1, shards)]
    if tuned:
        block = rows = own_rows
        numbers = [gathered_numbers(layout, GATHER_ORDER, 2, here, flag) for flag in (True, False)]
        place = jnp.stack(numbers) * own_rows
        chip = (numbers[1] // 4 * 2 + numbers[1] % 2)[::2]
        slots = [
            jnp.stack([slots_of(layout, order, here, flag) for flag in (True, False)])
            for order in REDUCE_ORDER
        ]
        slots = [
            slot // 2 * (2 * block + extra) + slot % 2 * block
            for slot, extra in zip(slots, (0, 16))
        ]
        halves = [
            jnp.concatenate([weight[:, s + h * n // 2 : s + (h + 1) * n // 2] for s, n in chunks], axis=1)
            for h in range(2)
        ]
        lane = jnp.where(
            here["x"] == 0, jnp.pad(bias, (0, 128 - own_rows)), jnp.pad(bias, (128 - own_rows, 0))
        )
        bias_block = jnp.broadcast_to(jnp.pad(lane, (0, width // 2 - 128))[None], (8, width // 2))
        ours = jnp.where(core == 0, halves[0], halves[1])
        theirs = layout.swap(
            jnp.concatenate([jnp.where(core == 0, halves[1], halves[0]), bias_block], axis=0)
        )
        half = chunks[0][1] // 2
        bases = [
            jnp.concatenate(
                [
                    ours[:, :half],
                    theirs[:own_rows, :half],
                    bias_block[:, :half],
                    theirs[own_rows:, :half],
                ],
                axis=0,
            )[None],
            jnp.concatenate([ours[:, half:], theirs[:own_rows, half:]], axis=0)[None],
        ]
        got_a = gather_step(layout, bases[0], GATHER_ORDER, 0)
    else:
        block = rows = 64
        place = jnp.zeros((2, 1), jnp.int32)
        chip = jnp.zeros((2,), jnp.int32)
        slots = [
            jnp.broadcast_to(jnp.arange(0, width, block, dtype=jnp.int32), (2, width // block))
        ] * 2
        theirs = weight
        wholes = [
            lax.all_gather(weight[:, start : start + size], BOTH, axis=0, tiled=True)
            for start, size in chunks
        ]
    tables = [array.astype(jnp.int32) for array in (place, chip, *slots, core.reshape(1))]
    neighbours, tables = tie((neighbours, tables), theirs)

    table = node_count + (3 * shards - 1) * rim
    shifted = neighbours - node_count
    section = shifted // span
    ahead = (shifted // rim % shards - here["x"]) % shards
    near_section = jnp.where(core == 0, 2, 1)
    base_slot = jnp.where(
        section == 0,
        node_count - rim,
        jnp.where(section == near_section, node_count + span - rim, node_count + 2 * span - rim),
    )
    slot = base_slot + ahead * rim + shifted % rim
    slot = jnp.where((section == 0) & (ahead == 0), shifted % rim, slot)
    codes = jnp.where(neighbours < node_count, neighbours, slot)
    degree = jnp.sum((neighbours >= 0).astype(F32), axis=2)
    alive = (jnp.arange(node_count, dtype=jnp.int32)[None, :] < live_count).astype(F32)
    weighting = alive / (degree + 1.0)
    total_nodes = micro_count * node_count
    alive_wide = jnp.broadcast_to(alive.reshape(total_nodes, 1), (total_nodes, 128))
    scale_wide = jnp.broadcast_to(weighting.reshape(total_nodes, 1), (total_nodes, 128))
    cnt, cnt_t = count_tables(codes, table)

    if tuned:
        current = jnp.concatenate(got_a)
        current, far_0, cross_1, cnt, cnt_t, alive_wide, scale_wide, base_b = lax.optimization_barrier(
            (current, far_0, cross_1, cnt, cnt_t, alive_wide, scale_wide, bases[1])
        )
        got_a = gather_step(layout, current, GATHER_ORDER, 1)
    hop = jnp.concatenate([rim_own[0], far_0[0]])
    hop = [from_shard(hop, shards - k) for k in range(1, shards)]
    cross_0 = [both[:rim] for both in hop]
    far_0 = far_0 + [both[rim:] for both in hop]
    group_1 = jnp.concatenate([rim_own[1]] + cross_1)
    far_1 = [far_swap(group_1)]
    near_1 = near_swap(group_1)

    if tuned:
        current = jnp.concatenate(got_a)
        current, cross_0, far_0, far_1, near_1, base_b = lax.optimization_barrier(
            (current, cross_0, far_0, far_1, near_1, base_b)
        )
        got_a = gather_step(layout, current, GATHER_ORDER, 2)
        got_b = gather_step(layout, base_b, GATHER_ORDER, 0)
    near_0 = near_swap(jnp.concatenate([rim_own[0]] + cross_0))

    if tuned:
        last_a, current = jnp.concatenate(got_a), jnp.concatenate(got_b)
        last_a, current, near_0 = lax.optimization_barrier((last_a, current, near_0))
        got_a = gather_step(layout, last_a, GATHER_ORDER, 3)
        others_a = [layout.swap(last_a)]
        got_b = gather_step(layout, current, GATHER_ORDER, 1)
    mixed, mixed_t, token = mix(
        cnt, scale_wide, features, [cross_0 + [near_0] + far_0, cross_1 + [near_1] + far_1]
    )

    if tuned:
        current = jnp.concatenate(got_b)
        got_a, others_a, current, token = lax.optimization_barrier(
            (got_a, others_a, current, token)
        )
        got_b = gather_step(layout, current, GATHER_ORDER, 2)
        others_a += [layout.swap(piece) for piece in got_a[1:]]
        gathered = [(others_a, got_a), None]
        bias_table = None
    else:
        gathered = [([whole], [whole]) for whole in wholes]
        bias_full = lax.all_gather(bias, BOTH, axis=0, tiled=True).astype(F32)
        bias_table = jnp.broadcast_to(bias_full.reshape(width // 128, 1, 128), (width // 128, 8, 128))

    cot_rows = cotangent.reshape(total_nodes, width)
    before = None
    grads, weights = [], []
    results = []
    for j, (start, size) in enumerate(chunks):
        half = size // 2
        last = j == len(chunks) - 1
        if tuned and j == 1:
            reduced, got_b, others_b, before = lax.optimization_barrier(
                ([results[0][1], recv], got_b, others_b, before)
            )
            sums = reduce_step(layout, reduced, back_a, 0)
            reduced_a = reduce_send(layout, reduced, sums, back_a, 0)
            others_b += [layout.swap(piece) for piece in got_b[1:]]
            gathered[1] = (others_b, got_b)
        pair = []
        for side in range(2):
            if tuned and j == 0 and side == 1:
                last_b = jnp.concatenate(got_b)
                last_b, before, pair = lax.optimization_barrier((last_b, before, pair))
                recv = layout.swap(pair[0])
                got_b = gather_step(layout, last_b, GATHER_ORDER, 3)
                others_b = [layout.swap(last_b)]
            if tuned and j == 1 and side == 1:
                reduced_a, before, pair = lax.optimization_barrier((reduced_a, before, pair))
                recv = layout.swap(pair[0])
                sums = reduce_step(layout, reduced_a, back_a, 1)
                reduced_a = reduce_send(layout, reduced_a, sums, back_a, 1)
            took = layer_half(
                start,
                half,
                side,
                tuned and last,
                [tables[0], tables[1], tables[2 + j], tables[4]],
                token,
                mixed,
                mixed_t,
                bias_table,
                cot_rows,
                alive_wide,
                gathered[j][side],
                gathered[j][1] if bias_table is None else [],
                rows,
                before,
                block,
            )
            act, out, bias_sums, grad_part, weight_part = took[:5]
            if len(took) == 6:
                bias_table = took[5]
            before = (bias_sums, act)
            grads.append(grad_part)
            weights.append(weight_part)
            if tuned:
                out = out.reshape(devices // 2, -1, half)
            pair.append(out)
        results.append(pair)

    sizes = [rim] * (shards - 1) + [span] + [rim] * shards
    if tuned:
        reduced_a, reduced_b, before = lax.optimization_barrier(
            (reduced_a, [results[1][1], recv], before)
        )
        sums_a = reduce_step(layout, reduced_a, back_a, 2)
        sums_b = reduce_step(layout, reduced_b, back_b, 0)
        reduced_a = reduce_send(layout, reduced_a, sums_a, back_a, 2)
        reduced_b = reduce_send(layout, reduced_b, sums_b, back_b, 0)
    grad = mixed_grad(scale_wide, grads, weights)
    parts = rim_grads(cnt_t, grad, sizes)
    if tuned:
        reduced_a, reduced_b, parts = lax.optimization_barrier((reduced_a, reduced_b, parts))
        sums_a = reduce_step(layout, reduced_a, back_a, 3)
        sums_b = reduce_step(layout, reduced_b, back_b, 1)
        reduced_a = reduce_send(layout, reduced_a, sums_a, back_a, 3)
        reduced_b = reduce_send(layout, reduced_b, sums_b, back_b, 1)
    cross, far = parts[: shards - 1], parts[shards:]
    near_back = near_swap(parts[shards - 1]).astype(F32)

    def toward(m, k):
        return cross[k - 1][m].astype(F32) + near_back[m, k * rim : (k + 1) * rim]

    hop_0 = [
        from_shard(jnp.concatenate([toward(0, k).astype(BF16), far[k][0]]), k)
        for k in range(1, shards)
    ]
    hop_1 = far_swap(jnp.concatenate([part[1] for part in far]))
    local, head = own_grads(cnt_t, grad, rim)

    if tuned:
        reduced_b, reduced_a, hop_0, hop_1, local, head = lax.optimization_barrier(
            (reduced_b, reduced_a, hop_0, hop_1, local, head)
        )
        sums_b = reduce_step(layout, reduced_b, back_b, 2)
        reduced_b = reduce_send(layout, reduced_b, sums_b, back_b, 2)
        sums_b = reduce_step(layout, reduced_b, back_b, 3)
        reduced_b = reduce_send(layout, reduced_b, sums_b, back_b, 3)
    far_sum = far[0][0].astype(F32) + sum(both[rim:].astype(F32) for both in hop_0)
    back_0 = far_swap(far_sum.astype(BF16)).astype(F32)
    hop_1 = hop_1.astype(F32)
    back_1 = [
        from_shard((toward(1, k) + hop_1[k * rim : (k + 1) * rim]).astype(BF16), k)
        for k in range(1, shards)
    ]
    sum_0 = head[0] + near_back[0, :rim] + sum(both[:rim].astype(F32) for both in hop_0) + back_0
    sum_1 = head[1] + near_back[1, :rim] + hop_1[:rim] + sum(both.astype(F32) for both in back_1)
    head = jnp.stack([sum_0, sum_1]).astype(BF16)
    feature_grad = lax.dynamic_update_slice(local, head, (0, 0, 0))

    weight_grads = []
    for j in range(2):
        if tuned:
            both = sum(part[0].astype(F32) for part in (reduced_a, reduced_b)[j])
            ours, theirs = both[:block], layout.swap(both[block:])
            low_half = jnp.where(core == 0, ours, theirs[:block])
            high_half = jnp.where(core == 0, theirs[:block], ours)
            if j == 1:
                sums = both[2 * block : 2 * block + 8, :128] + theirs[block + 8 :, :128]
                sums = jnp.sum(sums, axis=0)
                bias_out = jnp.where(here["x"] == 0, sums[:own_rows], sums[128 - own_rows :])
        else:
            send, keep = results[j]
            low_half, high_half = (
                lax.psum_scatter(
                    jnp.where(core == which, keep, send), BOTH, scatter_dimension=0, tiled=True
                ).astype(F32)
                for which in (0, 1)
            )
        weight_grads += [low_half, high_half]
    if not tuned:
        bias_sum = jnp.sum(before[0], axis=1).reshape(width)
        bias_out = lax.psum_scatter(bias_sum, BOTH, scatter_dimension=0, tiled=True)

    return (
        before[1].reshape(features.shape),
        feature_grad,
        jnp.concatenate(weight_grads, axis=1),
        bias_out,
    )


def solution(mesh):
    layout = Layout(mesh.shape["blk"], mesh.shape["shard"])
    rows = P(None, BOTH, None)
    return jax.shard_map(
        functools.partial(per_device, layout),
        mesh=mesh,
        in_specs=(rows, P(BOTH, None), P(BOTH), rows, rows, P(None, BOTH)),
        out_specs=(rows, rows, P(BOTH, None), P(BOTH)),
        check_vma=False,
    )
```

time: 286 us -> 193 us (0.67)
  waiting for transfers between devices: 106 us -> 67.7 us
  starting transfers between devices: 61.1 us -> 37.2 us
  local copies, waits for them, and re-layouts: 28.3 us -> 5.93 us
  Pallas kernels: 78.9 us -> 68.8 us
    ppermute x41 -> x25, starting transfers between devices: 55.9 us -> 18.2 us  [shift(): return lax.ppermute(value, BOTH, pairs)]
    ppermute x41 -> x25, waiting for transfers between devices: 85.3 us -> 60.9 us  [shift(): return lax.ppermute(value, BOTH, pairs)]
    unnamed x56 -> x52, local copies, waits for them, and re-layouts: 21.7 us -> 2.14 us
    ppermute x3 -> x4, waiting for transfers between devices: 20.7 us -> 4.03 us  [from_shard(): lax.ppermute(value, 'shard', [(i, (i + by) % count) for i in range(count)])]
    ppermute x2 -> x4, starting transfers between devices: 0.07 us -> 12.8 us  [far_swap(): lax.ppermute(value, 'blk', [(i, (i + (1 if i % 2 else -1)) % count) for i...]
    pallas_call x4 -> x7, Pallas kernels: 69.9 us -> 59.9 us  [the longest x4 37.7 us: layer_half(): pl.pallas_call(functools.partial(half_kernel, plan), in_specs=specs, out_...]
    convert_element_type x10 -> x13, other arithmetic: 2.21 us -> 5.28 us  [the longest x8 4.75 us: reduce_step(): sum((part[k * size:(k + 1) * size].astype(F32) for part in parts))]
    concatenate x8 -> x0, local copies, waits for them, and re-layouts: 3 us -> none  [the longest x4 1.79 us: gather_phases(): current = jnp.concatenate(got, axis=0)]
  transfers between devices with their start and end apart: 48 -> 36, of which waited for: 17 -> 17; matrix products, arithmetic and copies ran while one was open for 6% -> 5% of each run, Pallas kernels for 19% -> 31%
where the time goes in v2:
time: 193 us; the launch traced here: 192 us
  Pallas kernels  68.8 us (36%)
  waiting for transfers between devices  67.7 us (35%)
  starting transfers between devices  37.2 us (19%)
  other arithmetic  11 us (6%)
  local copies, waits for them, and re-layouts  5.93 us (3%)
    ppermute x25, waiting for transfers between devices, shift(): return lax.ppermute(value, BOTH, pairs)  60.9 us
    pallas_call x4, Pallas kernels, layer_half(): pl.pallas_call(functools.partial(half_kernel, plan), in_specs=specs, out_...  37.7 us
    ppermute x25, starting transfers between devices, shift(): return lax.ppermute(value, BOTH, pairs)  18.2 us
    ppermute x4, starting transfers between devices, far_swap(): lax.ppermute(value, 'blk', [(i, (i + (1 if i % 2 else -1)) % count) for i...  12.8 us
    pallas_call x1, Pallas kernels, mixed_grad(): pl.pallas_call(functools.partial(mixed_grad_kernel, len(grads)), in_specs...  9.18 us
    pallas_call x1, Pallas kernels, mix(): pl.pallas_call(functools.partial(mix_kernel, [len(group) for group in pie...  8.26 us
    pallas_call x1, Pallas kernels, own_grads(): pl.pallas_call(own_grad_kernel, grid=(micro, width // wide), in_specs=[pl...  5.61 us
    ppermute x4, starting transfers between devices, from_shard(): lax.ppermute(value, 'shard', [(i, (i + by) % count) for i in range(count)])  5.49 us
  transfers between devices with their start and end apart: 36, of which 17 were waited for; matrix products, arithmetic and copies ran while one was open for 5% of the time, Pallas kernels for 31%

profile of v2, /device:TPU:0, one launch (start us, length us, event | category | flops | bytes accessed | tf_op | source)
XLA Modules:
  0.0 192.5 jit_solution(6829649110896037260)
XLA Ops:
  4.2 5.7 %collective-permute-start.2 = (bf16[64,2048]{1,0:T(8,128)(2,1)S(1)}, bf16[64,2048]{1,0:T(8,128)(2,1)S(1)}, u32[]{:S(2)}, u32[]{:S(2)}) collective-permute-start(bf16[64,2048]{1,0:T(8,128)(2,1)S(1)} %get-tuple-element.233), channel_id=1, source_target_pairs={{0,30},{2,4},{4,2},{6,8},{8,6},{10,12},{12,10},{14,16},{16,14},{18... | collective-permute-start | bytes 786440 | tf_op jit(solution)/shard_map/ppermute | solution.py:470
  13.9 4.7 %count_tables.1 = (bf16[2,512,832]{2,1,0:T(8,128)(2,1)S(1)}, bf16[2,832,512]{2,1,0:T(8,128)(2,1)S(1)}) custom-call(s32[2,512,16]{2,1,0:T(8,128)S(1)} %fusion.4.code_ref), custom_call_target="tpu_custom_call" | custom-call | flops 6600000000 | tf_op jit(solution)/shard_map/count_tables/pallas_call | solution.py:61
  23.6 6.7 %collective-permute-done.4 = bf16[2,144,512]{2,1,0:T(8,128)(2,1)S(1)} collective-permute-done((bf16[2,144,512]{2,1,0:T(8,128)(2,1)S(1)}, bf16[2,144,512]{2,1,0:T(8,128)(2,1)S(1)}, u32[]{:S(2)}, u32[]{:S(2)}) %collective-permute-start.4) | collective-permute-done | bytes 294944 | tf_op jit(solution)/shard_map/ppermute | solution.py:452
  30.4 3.0 %collective-permute-done.5 = bf16[128,2048]{1,0:T(8,128)(2,1)S(1)} collective-permute-done((bf16[128,2048]{1,0:T(8,128)(2,1)S(1)}, bf16[128,2048]{1,0:T(8,128)(2,1)S(1)}, u32[]{:S(2)}, u32[]{:S(2)}) %collective-permute-start.5) | collective-permute-done | bytes 524320 | tf_op jit(solution)/shard_map/ppermute | solution.py:460
  33.4 2.7 %collective-permute-done.6.refs_6_ = bf16[128,2048]{1,0:T(8,128)(2,1)S(1)} collective-permute-done((bf16[128,2048]{1,0:T(8,128)(2,1)S(1)}, bf16[128,2048]{1,0:T(8,128)(2,1)S(1)}, u32[]{:S(2)}, u32[]{:S(2)}) %collective-permute-start.6) | collective-permute-done | bytes 524320 | tf_op jit(solution)/shard_map/ppermute | solution.py:470
  37.3 3.4 %collective-permute-start.9 = (bf16[1,128,512]{2,1,0:T(8,128)(2,1)S(1)}, bf16[1,128,512]{2,1,0:T(8,128)(2,1)S(1)}, u32[]{:S(2)}, u32[]{:S(2)}) collective-permute-start(bf16[1,128,512]{2,1,0:T(8,128)(2,1)S(1)} %maximum_bitcast_fusion.1), channel_id=1, source_target_pairs={{0,16},{1,17},{2,18},{3,19},{4,20},{5,21},{6,22},{7,23},{8,24},{9,... | collective-permute-start | bytes 393224 | tf_op jit(solution)/shard_map/ppermute | solution.py:452
  40.7 6.5 %collective-permute-done.9 = bf16[1,128,512]{2,1,0:T(8,128)(2,1)S(1)} collective-permute-done((bf16[1,128,512]{2,1,0:T(8,128)(2,1)S(1)}, bf16[1,128,512]{2,1,0:T(8,128)(2,1)S(1)}, u32[]{:S(2)}, u32[]{:S(2)}) %collective-permute-start.9) | collective-permute-done | bytes 131104 | tf_op jit(solution)/shard_map/ppermute | solution.py:452
  47.4 1.8 collective-permute-start.11
  49.4 8.3 %mix.1 = (bf16[1024,2048]{1,0:T(8,128)(2,1)S(1)}, bf16[2048,1024]{1,0:T(8,128)(2,1)S(1)}, f32[8,128]{1,0:T(8,128)S(1)}) custom-call(bf16[2,512,832]{2,1,0:T(8,128)(2,1)S(1)} %get-tuple-element.130.cnt_ref, f32[1024,128]{1,0:T(8,128)S(1)} %broadcast_in_dim.44.scale_ref.scale, bf16[2,512,2048]{2,1,0:T(8,128)(2,1)S(1)} %copy-done, ...), custom_call_target="tpu_custom_call" | custom-call | flops 6600000000 | tf_op jit(solution)/shard_map/mix/pallas_call | solution.py:111
  58.0 5.7 %collective-permute-done.11.refs_12_.refs_10_ = bf16[8,144,512]{2,1,0:T(8,128)(2,1)S(1)} collective-permute-done((bf16[8,144,512]{2,1,0:T(8,128)(2,1)S(1)}, bf16[8,144,512]{2,1,0:T(8,128)(2,1)S(1)}, u32[]{:S(2)}, u32[]{:S(2)}) %collective-permute-start.11) | collective-permute-done | bytes 1179680 | tf_op jit(solution)/shard_map/ppermute | solution.py:452
  64.7 8.3 %collective-permute-done.15 = bf16[4,128,512]{2,1,0:T(8,128)(2,1)S(1)} collective-permute-done((bf16[4,128,512]{2,1,0:T(8,128)(2,1)S(1)}, bf16[4,128,512]{2,1,0:T(8,128)(2,1)S(1)}, u32[]{:S(2)}, u32[]{:S(2)}) %collective-permute-start.15) | collective-permute-done | bytes 524320 | tf_op jit(solution)/shard_map/ppermute | solution.py:452
  74.2 9.2 %layer_half.4 = (bf16[1024,2048]{1,0:T(8,128)(2,1)}, bf16[2048,512]{1,0:T(8,128)(2,1)}, f32[16,8,128]{2,1,0:T(8,128)S(1)}, bf16[1024,512]{1,0:T(8,128)(2,1)S(1)}...) custom-call(s32[2,32]{1,0:T(2,128)S(1)} %add_multiply_fusion.refs_0_, s32[16]{0:T(128)S(1)} %slice.290.refs_1_, ...), custom_call_target="tpu_custom_call" | custom-call | flops 8800000000 | tf_op jit(solution)/shard_map/layer_half/pallas_call | solution.py:318
  83.5 1.8 collective-permute-start.17
  85.3 9.2 %layer_half.5 = (bf16[1024,2048]{1,0:T(8,128)(2,1)}, bf16[2048,512]{1,0:T(8,128)(2,1)}, f32[16,8,128]{2,1,0:T(8,128)S(1)}, bf16[1024,512]{1,0:T(8,128)(2,1)S(1)}, bf16[2048,512]{1,0:T(8,128)(2,1)S(1)}) custom-call(s32[2,32]{1,0:T(2,128)S(1)} %add_multiply_fusion.refs_0_, s32[16]{0:T(128)S(1)} %slice.290.refs_1_, ...), custom_call_target="tpu_custom_call", output_to_operand_aliasing={{0}: (13, {})} | custom-call | flops 8800000000 | tf_op jit(solution)/shard_map/layer_half/pallas_call | solution.py:318
  94.6 3.8 %collective-permute-done.17.refs_10_ = bf16[8,128,512]{2,1,0:T(8,128)(2,1)S(1)} collective-permute-done((bf16[8,128,512]{2,1,0:T(8,128)(2,1)S(1)}, bf16[8,128,512]{2,1,0:T(8,128)(2,1)S(1)}, u32[]{:S(2)}, u32[]{:S(2)}) %collective-permute-start.17) | collective-permute-done | bytes 1048608 | tf_op jit(solution)/shard_map/ppermute | solution.py:452
  98.4 2.2 %add_convert_fusion.1 = bf16[8,128,512]{2,1,0:T(8,128)(2,1)S(1)} fusion(bf16[16,128,512]{2,1,0:T(8,128)(2,1)S(1)} %collective-permute-done.16, bf16[16,128,512]{2,1,0:T(8,128)(2,1)} %bitcast.83), kind=kLoop, calls=%fused_computation.1 | loop fusion | flops 2097152 | bytes 3145728 | tf_op jit(solution)/shard_map/convert_element_type | solution.py:487
  102.8 9.5 %layer_half.6 = (bf16[1024,2048]{1,0:T(8,128)(2,1)}, bf16[2304,512]{1,0:T(8,128)(2,1)}, f32[16,8,128]{2,1,0:T(8,128)S(1)}, bf16[1024,512]{1,0:T(8,128)(2,1)S(1)}, bf16[2048,512]{1,0:T(8,128)(2,1)S(1)}) custom-call(s32[2,32]{1,0:T(2,128)S(1)} %add_multiply_fusion.refs_0_, s32[16]{0:T(128)S(1)} %slice.290.refs_1_, ...), custom_call_target="tpu_custom_call", output_to_operand_aliasing={{0}: (13, {})} | custom-call | flops 8800000000 | tf_op jit(solution)/shard_map/layer_half/pallas_call | solution.py:318
  112.2 3.3 %collective-permute-done.19 = bf16[8,128,512]{2,1,0:T(8,128)(2,1)S(1)} collective-permute-done((bf16[8,128,512]{2,1,0:T(8,128)(2,1)S(1)}, bf16[8,128,512]{2,1,0:T(8,128)(2,1)S(1)}, u32[]{:S(2)}, u32[]{:S(2)}) %collective-permute-start.19) | collective-permute-done | bytes 1048608 | tf_op jit(solution)/shard_map/ppermute | solution.py:452
  115.9 1.8 collective-permute-start.21
  117.7 9.8 %layer_half.7 = (bf16[1024,2048]{1,0:T(8,128)(2,1)}, bf16[2304,512]{1,0:T(8,128)(2,1)}, f32[16,8,128]{2,1,0:T(8,128)}, bf16[1024,512]{1,0:T(8,128)(2,1)S(1)}, bf16[2048,512]{1,0:T(8,128)(2,1)S(1)}) custom-call(s32[2,32]{1,0:T(2,128)S(1)} %add_multiply_fusion.refs_0_, s32[16]{0:T(128)S(1)} %slice.290.refs_1_, ...), custom_call_target="tpu_custom_call", output_to_operand_aliasing={{0}: (13, {})} | custom-call | flops 8800000000 | tf_op jit(solution)/shard_map/layer_half/pallas_call | solution.py:318
  127.5 1.6 add_convert_fusion
  130.0 9.2 %mixed_grad.1.grad_ref = bf16[1024,2048]{1,0:T(8,128)(2,1)S(1)} custom-call(f32[1024,128]{1,0:T(8,128)S(1)} %broadcast_in_dim.44.scale_ref.scale, bf16[1024,512]{1,0:T(8,128)(2,1)S(1)} %get-tuple-element.184.refs_0_, bf16[1024,512]{1,0:T(8,128)(2,1)S(1)} %get-tuple-element.185.refs_1_, bf16[1024,512]{1,0:T(8,128)(2,1)S(1)} %get-tuple-element.186.refs_2_, ...), custom_call_target="tpu_custom_call" | custom-call | flops 11000000512 | tf_op jit(solution)/shard_map/mixed_grad/pallas_call | solution.py:355
  139.5 3.4 %rim_grads.1 = (bf16[2,64,2048]{2,1,0:T(8,128)(2,1)S(1)}, bf16[2,128,2048]{2,1,0:T(8,128)(2,1)S(1)}, bf16[2,64,2048]{2,1,0:T(8,128)(2,1)S(1)}, bf16[2,64,2048]{2,1,0:T(8,128)(2,1)S(1)}) custom-call(bf16[2,832,512]{2,1,0:T(8,128)(2,1)S(1)} %get-tuple-element.183.cnt_t_ref, bf16[1024,2048]{1,0:T(8,128)(2,1)S(1)} %mixed_grad.1.grad_ref), custom_call_target="tpu_custom_call" | custom-call | flops 3300000000 | tf_op jit(solution)/shard_map/rim_grads/pallas_call | solution.py:379
  143.1 4.5 %collective-permute-done.23 = bf16[2,128,512]{2,1,0:T(8,128)(2,1)S(1)} collective-permute-done((bf16[2,128,512]{2,1,0:T(8,128)(2,1)S(1)}, bf16[2,128,512]{2,1,0:T(8,128)(2,1)S(1)}, u32[]{:S(2)}, u32[]{:S(2)}) %collective-permute-start.23) | collective-permute-done | bytes 262176 | tf_op jit(solution)/shard_map/ppermute | solution.py:452
  148.3 4.0 %collective-permute-start.29 = (bf16[128,2048]{1,0:T(8,128)(2,1)S(1)}, bf16[128,2048]{1,0:T(8,128)(2,1)S(1)}, u32[]{:S(2)}, u32[]{:S(2)}) collective-permute-start(bf16[128,2048]{1,0:T(8,128)(2,1)S(1)} %pad_maximum_fusion.8), channel_id=1, source_target_pairs={{0,30},{2,4},{4,2},{6,8},{8,6},{10,12},{12,10},{14,16},{16,14},{18... | collective-permute-start | bytes 1572872 | tf_op jit(solution)/shard_map/ppermute | solution.py:470
  155.0 5.6 %own_grads.1 = (bf16[2,512,2048]{2,1,0:T(8,128)(2,1)}, f32[2,64,2048]{2,1,0:T(8,128)S(1)}) custom-call(bf16[2,832,512]{2,1,0:T(8,128)(2,1)S(1)} %get-tuple-element.183.cnt_t_ref, bf16[1024,2048]{1,0:T(8,128)(2,1)S(1)} %mixed_grad.1.grad_ref), custom_call_target="tpu_custom_call" | custom-call | flops 4400000000 | tf_op jit(solution)/shard_map/own_grads/pallas_call | solution.py:404
  160.8 3.4 %collective-permute-done.26 = bf16[1,128,512]{2,1,0:T(8,128)(2,1)S(1)} collective-permute-done((bf16[1,128,512]{2,1,0:T(8,128)(2,1)S(1)}, bf16[1,128,512]{2,1,0:T(8,128)(2,1)S(1)}, u32[]{:S(2)}, u32[]{:S(2)}) %collective-permute-start.26) | collective-permute-done | bytes 131104 | tf_op jit(solution)/shard_map/ppermute | solution.py:452
  164.2 1.9 collective-permute-done.25
  167.2 3.0 %collective-permute-start.30 = (bf16[64,2048]{1,0:T(8,128)(2,1)S(1)}, bf16[64,2048]{1,0:T(8,128)(2,1)S(1)}, u32[]{:S(2)}, u32[]{:S(2)}) collective-permute-start(bf16[64,2048]{1,0:T(8,128)(2,1)S(1)} %fusion.15), channel_id=1, source_target_pairs={{0,30},{2,4},{4,2},{6,8},{8,6},{10,12},{12,10},{14,16},{16,14},{18... | collective-permute-start | bytes 786440 | tf_op jit(solution)/shard_map/ppermute | solution.py:470
  172.2 7.6 %collective-permute-done.33 = bf16[2,144,512]{2,1,0:T(8,128)(2,1)S(1)} collective-permute-done((bf16[2,144,512]{2,1,0:T(8,128)(2,1)S(1)}, bf16[2,144,512]{2,1,0:T(8,128)(2,1)S(1)}, u32[]{:S(2)}, u32[]{:S(2)}) %collective-permute-start.33) | collective-permute-done | bytes 294944 | tf_op jit(solution)/shard_map/ppermute | solution.py:452
  180.0 2.3 %collective-permute-start.34 = (bf16[1,144,512]{2,1,0:T(8,128)(2,1)S(1)}, bf16[1,144,512]{2,1,0:T(8,128)(2,1)S(1)}, u32[]{:S(2)}, u32[]{:S(2)}) collective-permute-start(bf16[1,144,512]{2,1,0:T(8,128)(2,1)S(1)} %add_convert_fusion.6), channel_id=1, source_target_pairs={{0,16},{1,17},{2,18},{3,19},{4,20},{5,21},{6,22},{7,23},{8,24},{9,... | collective-permute-start | bytes 442376 | tf_op jit(solution)/shard_map/ppermute | solution.py:452
  182.6 6.9 %collective-permute-done.34 = bf16[1,144,512]{2,1,0:T(8,128)(2,1)S(1)} collective-permute-done((bf16[1,144,512]{2,1,0:T(8,128)(2,1)S(1)}, bf16[1,144,512]{2,1,0:T(8,128)(2,1)S(1)}, u32[]{:S(2)}, u32[]{:S(2)}) %collective-permute-start.34) | collective-permute-done | bytes 147488 | tf_op jit(solution)/shard_map/ppermute | solution.py:452
  (195 shorter events, 29.9 us)
Async XLA Ops:
  2.7 9.2 %collective-permute-start = (bf16[72,1024]{1,0:T(8,128)(2,1)S(1)}, bf16[72,1024]{1,0:T(8,128)(2,1)S(1)}, u32[]{:S(2)}, u32[]{:S(2)}) collective-permute-start(bf16[72,1024]{1,0:T(8,128)(2,1)S(1)} %pad_maximum_fusion.12), channel_id=1, source_target_pairs={{0,2},{1,3},{2,0},{3,1},{4,6},{5,7},{6,4},{7,5},{8,10},{9,11},{10,... | collective-permute-start | bytes 442376 | tf_op jit(solution)/shard_map/ppermute | solution.py:452
  4.2 15.9 %collective-permute-start.2 = (bf16[64,2048]{1,0:T(8,128)(2,1)S(1)}, bf16[64,2048]{1,0:T(8,128)(2,1)S(1)}, u32[]{:S(2)}, u32[]{:S(2)}) collective-permute-start(bf16[64,2048]{1,0:T(8,128)(2,1)S(1)} %get-tuple-element.233), channel_id=1, source_target_pairs={{0,30},{2,4},{4,2},{6,8},{8,6},{10,12},{12,10},{14,16},{16,14},{18... | collective-permute-start | bytes 786440 | tf_op jit(solution)/shard_map/ppermute | solution.py:470
  10.0 10.2 %collective-permute-start.3 = (bf16[64,2048]{1,0:T(8,128)(2,1)S(1)}, bf16[64,2048]{1,0:T(8,128)(2,1)S(1)}, u32[]{:S(2)}, u32[]{:S(2)}) collective-permute-start(bf16[64,2048]{1,0:T(8,128)(2,1)S(1)} %get-tuple-element.232), channel_id=1, source_target_pairs={{0,1},{1,0},{2,3},{3,2},{4,5},{5,4},{6,7},{7,6},{8,9},{9,8},{10,11... | collective-permute-start | bytes 786440 | tf_op jit(solution)/shard_map/ppermute | solution.py:460
  12.2 7.9 %collective-permute-start.1 = (bf16[1,144,512]{2,1,0:T(8,128)(2,1)S(1)}, bf16[1,144,512]{2,1,0:T(8,128)(2,1)S(1)}, u32[]{:S(2)}, u32[]{:S(2)}) collective-permute-start(bf16[1,144,512]{2,1,0:T(8,128)(2,1)S(1)} %maximum_bitcast_fusion), channel_id=1, source_target_pairs={{0,16},{1,17},{2,18},{3,19},{4,20},{5,21},{6,22},{7,23},{8,24},{9,... | collective-permute-start | bytes 442376 | tf_op jit(solution)/shard_map/ppermute | solution.py:452
  20.6 12.8 %collective-permute-start.5 = (bf16[128,2048]{1,0:T(8,128)(2,1)S(1)}, bf16[128,2048]{1,0:T(8,128)(2,1)S(1)}, u32[]{:S(2)}, u32[]{:S(2)}) collective-permute-start(bf16[128,2048]{1,0:T(8,128)(2,1)S(1)} %pad_maximum_fusion.3), channel_id=1, source_target_pairs={{0,1},{1,0},{2,3},{3,2},{4,5},{5,4},{6,7},{7,6},{8,9},{9,8},{10,11... | collective-permute-start | bytes 1572872 | tf_op jit(solution)/shard_map/ppermute | solution.py:460
  22.1 8.2 %collective-permute-start.4 = (bf16[2,144,512]{2,1,0:T(8,128)(2,1)S(1)}, bf16[2,144,512]{2,1,0:T(8,128)(2,1)S(1)}, u32[]{:S(2)}, u32[]{:S(2)}) collective-permute-start(bf16[2,144,512]{2,1,0:T(8,128)(2,1)S(1)} %pad_maximum_fusion.10), channel_id=1, source_target_pairs={{0,8},{1,9},{2,10},{3,11},{4,12},{5,13},{6,14},{7,15},{8,0},{9,1},... | collective-permute-start | bytes 884744 | tf_op jit(solution)/shard_map/ppermute | solution.py:452
  23.4 12.7 %collective-permute-start.6 = (bf16[128,2048]{1,0:T(8,128)(2,1)S(1)}, bf16[128,2048]{1,0:T(8,128)(2,1)S(1)}, u32[]{:S(2)}, u32[]{:S(2)}) collective-permute-start(bf16[128,2048]{1,0:T(8,128)(2,1)S(1)} %pad_maximum_fusion.5), channel_id=1, source_target_pairs={{0,30},{2,4},{4,2},{6,8},{8,6},{10,12},{12,10},{14,16},{16,14},{18... | collective-permute-start | bytes 1572872 | tf_op jit(solution)/shard_map/ppermute | solution.py:470
  23.5 12.6 %collective-permute-start.7 = (bf16[128,2048]{1,0:T(8,128)(2,1)S(1)}, bf16[128,2048]{1,0:T(8,128)(2,1)S(1)}, u32[]{:S(2)}, u32[]{:S(2)}) collective-permute-start(bf16[128,2048]{1,0:T(8,128)(2,1)S(1)} %pad_maximum_fusion.5), channel_id=1, source_target_pairs={{0,2},{2,0},{4,6},{6,4},{8,10},{10,8},{12,14},{14,12},{16,18},{18,... | collective-permute-start | bytes 1572872 | tf_op jit(solution)/shard_map/ppermute | solution.py:465
  36.1 11.1 %collective-permute-start.8 = (bf16[4,144,512]{2,1,0:T(8,128)(2,1)S(1)}, bf16[4,144,512]{2,1,0:T(8,128)(2,1)S(1)}, u32[]{:S(2)}, u32[]{:S(2)}) collective-permute-start(bf16[4,144,512]{2,1,0:T(8,128)(2,1)S(1)} %pad_maximum_fusion.4), channel_id=1, source_target_pairs={{0,1},{1,0},{2,6},{3,7},{4,5},{5,4},{6,2},{7,3},{8,9},{9,8},{10,14... | collective-permute-start | bytes 1769480 | tf_op jit(solution)/shard_map/ppermute | solution.py:452
  36.6 10.8 %collective-permute-start.10 = (bf16[128,2048]{1,0:T(8,128)(2,1)S(1)}, bf16[128,2048]{1,0:T(8,128)(2,1)S(1)}, u32[]{:S(2)}, u32[]{:S(2)}) collective-permute-start(bf16[128,2048]{1,0:T(8,128)(2,1)S(1)} %pad_maximum_fusion.2), channel_id=1, source_target_pairs={{0,2},{2,0},{4,6},{6,4},{8,10},{10,8},{12,14},{14,12},{16,18},{18,... | collective-permute-start | bytes 1572872 | tf_op jit(solution)/shard_map/ppermute | solution.py:465
  37.3 9.9 %collective-permute-start.9 = (bf16[1,128,512]{2,1,0:T(8,128)(2,1)S(1)}, bf16[1,128,512]{2,1,0:T(8,128)(2,1)S(1)}, u32[]{:S(2)}, u32[]{:S(2)}) collective-permute-start(bf16[1,128,512]{2,1,0:T(8,128)(2,1)S(1)} %maximum_bitcast_fusion.1), channel_id=1, source_target_pairs={{0,16},{1,17},{2,18},{3,19},{4,20},{5,21},{6,22},{7,23},{8,24},{9,... | collective-permute-start | bytes 393224 | tf_op jit(solution)/shard_map/ppermute | solution.py:452
  47.4 16.3 %collective-permute-start.11 = (bf16[8,144,512]{2,1,0:T(8,128)(2,1)S(1)}, bf16[8,144,512]{2,1,0:T(8,128)(2,1)S(1)}, u32[]{:S(2)}, u32[]{:S(2)}) collective-permute-start(bf16[8,144,512]{2,1,0:T(8,128)(2,1)S(1)} %pad_maximum_fusion.refs_11_.refs_9_), channel_id=1, source_target_pairs={{0,4},{1,5},{2,3},{3,2},{4,0},{5,1},{6,7},{7,6},{8,12},{9,13},{10,... | collective-permute-start | bytes 3538952 | tf_op jit(solution)/shard_map/ppermute | solution.py:452
  49.2 14.5 %collective-permute-start.12 = (bf16[8,144,512]{2,1,0:T(8,128)(2,1)S(1)}, bf16[8,144,512]{2,1,0:T(8,128)(2,1)S(1)}, u32[]{:S(2)}, u32[]{:S(2)}) collective-permute-start(bf16[8,144,512]{2,1,0:T(8,128)(2,1)S(1)} %pad_maximum_fusion.refs_11_.refs_9_), channel_id=1, source_target_pairs={{0,2},{1,3},{2,0},{3,1},{4,6},{5,7},{6,4},{7,5},{8,10},{9,11},{10,... | collective-permute-start | bytes 3538952 | tf_op jit(solution)/shard_map/ppermute | solution.py:452
  49.2 8.7 %collective-permute-start.13 = (bf16[2,128,512]{2,1,0:T(8,128)(2,1)S(1)}, bf16[2,128,512]{2,1,0:T(8,128)(2,1)S(1)}, u32[]{:S(2)}, u32[]{:S(2)}) collective-permute-start(bf16[2,128,512]{2,1,0:T(8,128)(2,1)S(1)} %pad_maximum_fusion.11), channel_id=1, source_target_pairs={{0,8},{1,9},{2,10},{3,11},{4,12},{5,13},{6,14},{7,15},{8,0},{9,1},... | collective-permute-start | bytes 786440 | tf_op jit(solution)/shard_map/ppermute | solution.py:452
  63.7 9.4 %collective-permute-start.14 = (bf16[8,144,512]{2,1,0:T(8,128)(2,1)S(1)}, bf16[8,144,512]{2,1,0:T(8,128)(2,1)S(1)}, u32[]{:S(2)}, u32[]{:S(2)}) collective-permute-start(bf16[8,144,512]{2,1,0:T(8,128)(2,1)S(1)} %collective-permute-done.11.refs_12_.refs_10_), channel_id=1, source_target_pairs={{0,2},{1,3},{2,0},{3,1},{4,6},{5,7},{6,4},{7,5},{8,10},{9,11},{10,... | collective-permute-start | bytes 3538952 | tf_op jit(solution)/shard_map/ppermute | solution.py:452
  63.7 9.2 %collective-permute-start.15 = (bf16[4,128,512]{2,1,0:T(8,128)(2,1)S(1)}, bf16[4,128,512]{2,1,0:T(8,128)(2,1)S(1)}, u32[]{:S(2)}, u32[]{:S(2)}) collective-permute-start(bf16[4,128,512]{2,1,0:T(8,128)(2,1)S(1)} %pad_maximum_fusion.6), channel_id=1, source_target_pairs={{0,1},{1,0},{2,6},{3,7},{4,5},{5,4},{6,2},{7,3},{8,9},{9,8},{10,14... | collective-permute-start | bytes 1572872 | tf_op jit(solution)/shard_map/ppermute | solution.py:452
  83.4 15.0 %collective-permute-start.16 = (bf16[16,128,512]{2,1,0:T(8,128)(2,1)}, bf16[16,128,512]{2,1,0:T(8,128)(2,1)S(1)}, u32[]{:S(2)}, u32[]{:S(2)}) collective-permute-start(bf16[16,128,512]{2,1,0:T(8,128)(2,1)} %bitcast.96), channel_id=1, source_target_pairs={{0,2},{1,3},{2,0},{3,1},{4,6},{5,7},{6,4},{7,5},{8,10},{9,11},{10,... | collective-permute-start | bytes 6291464 | tf_op jit(solution)/shard_map/ppermute | solution.py:452
  83.5 14.9 %collective-permute-start.17 = (bf16[8,128,512]{2,1,0:T(8,128)(2,1)S(1)}, bf16[8,128,512]{2,1,0:T(8,128)(2,1)S(1)}, u32[]{:S(2)}, u32[]{:S(2)}) collective-permute-start(bf16[8,128,512]{2,1,0:T(8,128)(2,1)S(1)} %pad_maximum_fusion.1.refs_9_), channel_id=1, source_target_pairs={{0,4},{1,5},{2,3},{3,2},{4,0},{5,1},{6,7},{7,6},{8,12},{9,13},{10,... | collective-permute-start | bytes 3145736 | tf_op jit(solution)/shard_map/ppermute | solution.py:452
  85.3 13.1 %collective-permute-start.18 = (bf16[8,128,512]{2,1,0:T(8,128)(2,1)S(1)}, bf16[8,128,512]{2,1,0:T(8,128)(2,1)S(1)}, u32[]{:S(2)}, u32[]{:S(2)}) collective-permute-start(bf16[8,128,512]{2,1,0:T(8,128)(2,1)S(1)} %pad_maximum_fusion.1.refs_9_), channel_id=1, source_target_pairs={{0,2},{1,3},{2,0},{3,1},{4,6},{5,7},{6,4},{7,5},{8,10},{9,11},{10,... | collective-permute-start | bytes 3145736 | tf_op jit(solution)/shard_map/ppermute | solution.py:452
  100.7 14.9 %collective-permute-start.19 = (bf16[8,128,512]{2,1,0:T(8,128)(2,1)S(1)}, bf16[8,128,512]{2,1,0:T(8,128)(2,1)S(1)}, u32[]{:S(2)}, u32[]{:S(2)}) collective-permute-start(bf16[8,128,512]{2,1,0:T(8,128)(2,1)S(1)} %add_convert_fusion.1), channel_id=1, source_target_pairs={{0,1},{1,0},{2,6},{3,7},{4,5},{5,4},{6,2},{7,3},{8,9},{9,8},{10,14... | collective-permute-start | bytes 3145736 | tf_op jit(solution)/shard_map/ppermute | solution.py:452
  115.5 12.0 %collective-permute-start.22 = (bf16[16,144,512]{2,1,0:T(8,128)(2,1)}, bf16[16,144,512]{2,1,0:T(8,128)(2,1)S(1)}, u32[]{:S(2)}, u32[]{:S(2)}) collective-permute-start(bf16[16,144,512]{2,1,0:T(8,128)(2,1)} %bitcast.95), channel_id=1, source_target_pairs={{0,2},{1,3},{2,0},{3,1},{4,6},{5,7},{6,4},{7,5},{8,10},{9,11},{10,... | collective-permute-start | bytes 7077896 | tf_op jit(solution)/shard_map/ppermute | solution.py:452
  115.9 11.6 %collective-permute-start.21 = (bf16[4,128,512]{2,1,0:T(8,128)(2,1)S(1)}, bf16[4,128,512]{2,1,0:T(8,128)(2,1)S(1)}, u32[]{:S(2)}, u32[]{:S(2)}) collective-permute-start(bf16[4,128,512]{2,1,0:T(8,128)(2,1)S(1)} %add_convert_fusion.3), channel_id=1, source_target_pairs={{0,4},{1,5},{2,3},{3,2},{4,0},{5,1},{6,7},{7,6},{8,12},{9,13},{10,... | collective-permute-start | bytes 1572872 | tf_op jit(solution)/shard_map/ppermute | solution.py:452
  129.1 18.5 %collective-permute-start.24 = (bf16[8,144,512]{2,1,0:T(8,128)(2,1)S(1)}, bf16[8,144,512]{2,1,0:T(8,128)(2,1)S(1)}, u32[]{:S(2)}, u32[]{:S(2)}) collective-permute-start(bf16[8,144,512]{2,1,0:T(8,128)(2,1)S(1)} %add_convert_fusion), channel_id=1, source_target_pairs={{0,1},{1,0},{2,6},{3,7},{4,5},{5,4},{6,2},{7,3},{8,9},{9,8},{10,14... | collective-permute-start | bytes 3538952 | tf_op jit(solution)/shard_map/ppermute | solution.py:452
  139.4 8.2 %collective-permute-start.23 = (bf16[2,128,512]{2,1,0:T(8,128)(2,1)S(1)}, bf16[2,128,512]{2,1,0:T(8,128)(2,1)S(1)}, u32[]{:S(2)}, u32[]{:S(2)}) collective-permute-start(bf16[2,128,512]{2,1,0:T(8,128)(2,1)S(1)} %add_convert_fusion.5), channel_id=1, source_target_pairs={{0,8},{1,9},{2,10},{3,11},{4,12},{5,13},{6,14},{7,15},{8,0},{9,1},... | collective-permute-start | bytes 786440 | tf_op jit(solution)/shard_map/ppermute | solution.py:452
  147.8 18.3 %collective-permute-start.25 = (bf16[4,144,512]{2,1,0:T(8,128)(2,1)S(1)}, bf16[4,144,512]{2,1,0:T(8,128)(2,1)S(1)}, u32[]{:S(2)}, u32[]{:S(2)}) collective-permute-start(bf16[4,144,512]{2,1,0:T(8,128)(2,1)S(1)} %add_convert_fusion.2), channel_id=1, source_target_pairs={{0,4},{1,5},{2,3},{3,2},{4,0},{5,1},{6,7},{7,6},{8,12},{9,13},{10,... | collective-permute-start | bytes 1769480 | tf_op jit(solution)/shard_map/ppermute | solution.py:452
  148.3 15.9 %collective-permute-start.29 = (bf16[128,2048]{1,0:T(8,128)(2,1)S(1)}, bf16[128,2048]{1,0:T(8,128)(2,1)S(1)}, u32[]{:S(2)}, u32[]{:S(2)}) collective-permute-start(bf16[128,2048]{1,0:T(8,128)(2,1)S(1)} %pad_maximum_fusion.8), channel_id=1, source_target_pairs={{0,30},{2,4},{4,2},{6,8},{8,6},{10,12},{12,10},{14,16},{16,14},{18... | collective-permute-start | bytes 1572872 | tf_op jit(solution)/shard_map/ppermute | solution.py:470
  152.7 14.5 %collective-permute-start.28 = (bf16[128,2048]{1,0:T(8,128)(2,1)S(1)}, bf16[128,2048]{1,0:T(8,128)(2,1)S(1)}, u32[]{:S(2)}, u32[]{:S(2)}) collective-permute-start(bf16[128,2048]{1,0:T(8,128)(2,1)S(1)} %pad_maximum_fusion.7), channel_id=1, source_target_pairs={{0,1},{1,0},{2,3},{3,2},{4,5},{5,4},{6,7},{7,6},{8,9},{9,8},{10,11... | collective-permute-start | bytes 1572872 | tf_op jit(solution)/shard_map/ppermute | solution.py:460
  154.0 10.2 %collective-permute-start.26 = (bf16[1,128,512]{2,1,0:T(8,128)(2,1)S(1)}, bf16[1,128,512]{2,1,0:T(8,128)(2,1)S(1)}, u32[]{:S(2)}, u32[]{:S(2)}) collective-permute-start(bf16[1,128,512]{2,1,0:T(8,128)(2,1)S(1)} %add_convert_fusion.7), channel_id=1, source_target_pairs={{0,16},{1,17},{2,18},{3,19},{4,20},{5,21},{6,22},{7,23},{8,24},{9,... | collective-permute-start | bytes 393224 | tf_op jit(solution)/shard_map/ppermute | solution.py:452
  167.2 15.1 %collective-permute-start.30 = (bf16[64,2048]{1,0:T(8,128)(2,1)S(1)}, bf16[64,2048]{1,0:T(8,128)(2,1)S(1)}, u32[]{:S(2)}, u32[]{:S(2)}) collective-permute-start(bf16[64,2048]{1,0:T(8,128)(2,1)S(1)} %fusion.15), channel_id=1, source_target_pairs={{0,30},{2,4},{4,2},{6,8},{8,6},{10,12},{12,10},{14,16},{16,14},{18... | collective-permute-start | bytes 786440 | tf_op jit(solution)/shard_map/ppermute | solution.py:470
  170.5 9.3 %collective-permute-start.33 = (bf16[2,144,512]{2,1,0:T(8,128)(2,1)S(1)}, bf16[2,144,512]{2,1,0:T(8,128)(2,1)S(1)}, u32[]{:S(2)}, u32[]{:S(2)}) collective-permute-start(bf16[2,144,512]{2,1,0:T(8,128)(2,1)S(1)} %add_convert_fusion.4), channel_id=1, source_target_pairs={{0,8},{1,9},{2,10},{3,11},{4,12},{5,13},{6,14},{7,15},{8,0},{9,1},... | collective-permute-start | bytes 884744 | tf_op jit(solution)/shard_map/ppermute | solution.py:452
  171.0 11.3 %collective-permute-start.31 = (bf16[64,2048]{1,0:T(8,128)(2,1)S(1)}, bf16[64,2048]{1,0:T(8,128)(2,1)S(1)}, u32[]{:S(2)}, u32[]{:S(2)}) collective-permute-start(bf16[64,2048]{1,0:T(8,128)(2,1)S(1)} %fusion.5), channel_id=1, source_target_pairs={{0,1},{1,0},{2,3},{3,2},{4,5},{5,4},{6,7},{7,6},{8,9},{9,8},{10,11... | collective-permute-start | bytes 786440 | tf_op jit(solution)/shard_map/ppermute | solution.py:460
  180.0 9.4 %collective-permute-start.34 = (bf16[1,144,512]{2,1,0:T(8,128)(2,1)S(1)}, bf16[1,144,512]{2,1,0:T(8,128)(2,1)S(1)}, u32[]{:S(2)}, u32[]{:S(2)}) collective-permute-start(bf16[1,144,512]{2,1,0:T(8,128)(2,1)S(1)} %add_convert_fusion.6), channel_id=1, source_target_pairs={{0,16},{1,17},{2,18},{3,19},{4,20},{5,21},{6,22},{7,23},{8,24},{9,... | collective-permute-start | bytes 442376 | tf_op jit(solution)/shard_map/ppermute | solution.py:452
  (34 other events, 318.8 us)
